TPU v7x, 256 devices: a whole 4x4x8 slice. The times are simulated.
256 devices in a mesh: section: 4 (over z_lo), tile: 64 (over x, z_hi, y, core).
Axes of the slice: x: 4, y: 4, z: 8 (z_hi: 2, z_lo: 4; z = z_hi * 4 + z_lo), core: 2. Of those that a mesh axis runs over, the one named last changes fastest.
Arguments:
- saved_inputs: bfloat16 [4, 8, 64, 4, 8, 256], P('section', None, 'tile'), may hold values from -300 to 300
- cotangent: bfloat16 [8, 64, 4, 8, 256], P(None, 'tile'), may hold values from -6 to 6
- kernels: bfloat16 [4, 6912, 256], P('section'), may hold values from -0.078125 to 0.078125
- gains: float32 [4, 256], P('section'), may hold values from 0.1 to 1.9
- biases: float32 [4, 256], P('section'), may hold values from -3 to 3
Outputs:
- input_grads: bfloat16 [4, 8, 64, 4, 8, 256], P('section', None, 'tile')
- kernel_grads: float32 [4, 6912, 256], P('section', 'tile')
- gain_grads: float32 [4, 256], P('section')
- bias_grads: float32 [4, 256], P('section')
All inputs are finite; a program needn't handle non-finite values.
Results may differ from a plain program's by a relative error of at most 0.0055.
Values may be sent and summed in bfloat16 or wider, within the bound.
A program may use at most 128 MiB of HBM per device.

v0:
```python
import math

import jax
import jax.numpy as jnp
from jax import lax
from jax.sharding import PartitionSpec as P

GROUPS = 32
GRID_COLS = 8
SLICE = 8


NORM_EPSILON = 1e-05


def passed_along(value, axis, steps):
    count = lax.axis_size(axis)
    first, last = (max(0, -steps), min(count, count - steps))
    return lax.ppermute(value, axis, [(source, source + steps) for source in range(first, last)])


def rim_active(field, col_pos):
    from_left = passed_along(field[:, :, -1:, :], "tile", 1)
    from_right = passed_along(field[:, :, :1, :], "tile", -1)
    from_left = jnp.where(col_pos > 0, from_left, jnp.zeros_like(from_left))
    from_right = jnp.where(col_pos < GRID_COLS - 1, from_right, jnp.zeros_like(from_right))
    widened = jnp.concatenate([from_left, field, from_right], axis=2)
    from_above = passed_along(widened[:, -1:], "tile", GRID_COLS)
    from_below = passed_along(widened[:, :1], "tile", -GRID_COLS)
    return jnp.concatenate([from_above, widened, from_below], axis=1)


def rim_seed(field, col_pos):
    from_left = passed_along(field[:, :, -1:, :], "tile", 1)
    from_right = passed_along(field[:, :, :1, :], "tile", -1)
    from_left = jnp.where(col_pos > 0, from_left, jnp.zeros_like(from_left))
    from_right = jnp.where(col_pos < GRID_COLS - 1, from_right, jnp.zeros_like(from_right))
    widened = jnp.concatenate([from_left, field, from_right], axis=2)
    from_above = passed_along(widened[:, -1:], "tile", GRID_COLS)
    from_below = passed_along(widened[:, :1], "tile", -GRID_COLS)
    return jnp.concatenate([from_above, widened, from_below], axis=1)


def tap_columns(extended, length, tile_rows, tile_cols, flipped):
    pieces = []
    for tap_t in range(3):
        for tap_y in range(3):
            for tap_x in range(3):
                if flipped:
                    off_t, off_y, off_x = (2 - tap_t, 2 - tap_y, 2 - tap_x)
                else:
                    off_t, off_y, off_x = (tap_t, tap_y, tap_x)
                window = extended[
                    off_t : off_t + length, off_y : off_y + tile_rows, off_x : off_x + tile_cols
                ]
                pieces.append(window.reshape(length * tile_rows * tile_cols, -1))
    return jnp.concatenate(pieces, axis=1)


def on_device(saved_inputs, cotangent, kernels, gains, biases):
    frames = saved_inputs.shape[1]
    tile_rows = saved_inputs.shape[3]
    tile_cols = saved_inputs.shape[4]
    channels = saved_inputs.shape[5]
    per_group = channels // GROUPS
    sections = lax.axis_size("section")
    tile_count = lax.axis_size("tile")
    section_index = lax.axis_index("section")
    col_pos = lax.axis_index("tile") % GRID_COLS
    entry_count = float(tile_count * tile_rows * tile_cols * per_group)
    scale = 1.0 / math.sqrt(frames * tile_count * tile_rows * tile_cols)
    inputs = saved_inputs[0, :, 0]
    seeds = cotangent[:, 0]
    kernel = kernels[0]
    gain_row = gains[0]
    bias_row = biases[0]
    kernel_flip = (
        kernel.reshape(27, channels, channels).transpose(0, 2, 1).reshape(27 * channels, channels)
    )
    grouped = inputs.astype(jnp.float32).reshape(frames, tile_rows * tile_cols, GROUPS, per_group)
    total, squares = lax.psum(
        (jnp.sum(grouped, axis=(1, 3)), jnp.sum(grouped * grouped, axis=(1, 3))), "tile"
    )
    group_mean = total / entry_count
    rstd = lax.rsqrt(squares / entry_count - group_mean * group_mean + NORM_EPSILON)
    normed = ((grouped - group_mean[:, None, :, None]) * rstd[:, None, :, None]).reshape(
        frames, tile_rows, tile_cols, channels
    )
    hidden = normed * gain_row + bias_row
    active = jax.nn.silu(hidden).astype(jnp.bfloat16)
    active_rim = rim_active(active, col_pos)
    leading = jnp.zeros((2, tile_rows + 2, tile_cols + 2, channels), jnp.bfloat16)
    padded_active = jnp.concatenate([leading, active_rim], axis=0)
    frame_block = SLICE
    block_count = frames // frame_block
    tick_count = block_count + sections - 1
    is_last = section_index == sections - 1
    store = jnp.zeros((27 * channels, channels), jnp.float32)
    incoming = jnp.zeros((frame_block, tile_rows, tile_cols, channels), jnp.bfloat16)
    cache = jnp.zeros((2, tile_rows + 2, tile_cols + 2, channels), jnp.bfloat16)
    grads_out = jnp.zeros((frames, tile_rows, tile_cols, channels), jnp.bfloat16)
    gain_acc = jnp.zeros((channels,), jnp.float32)
    bias_acc = jnp.zeros((channels,), jnp.float32)

    def one_tick(tick_step, loop_state):
        incoming, cache, grads_out, store, gain_acc, bias_acc = loop_state
        block_pos = block_count - 1 - tick_step + (sections - 1 - section_index)
        is_valid = (block_pos >= 0) & (block_pos < block_count)
        seed_grad = jnp.where(is_last, seeds, incoming)
        seed_rim = rim_seed(seed_grad, col_pos)
        extended = jnp.concatenate([seed_rim, cache], axis=0)
        grad_active = jnp.dot(
            tap_columns(extended, frame_block, tile_rows, tile_cols, True),
            kernel_flip,
            preferred_element_type=jnp.float32,
        ).reshape(frame_block, tile_rows, tile_cols, channels)
        sigmoid_h = jax.nn.sigmoid(hidden)
        grad_hidden = grad_active * sigmoid_h * (1.0 + hidden * (1.0 - sigmoid_h))
        weighted = (grad_hidden * gain_row).reshape(
            frame_block, tile_rows * tile_cols, GROUPS, per_group
        )
        normed_g = normed.reshape(frame_block, tile_rows * tile_cols, GROUPS, per_group)
        first, second = lax.psum(
            (jnp.sum(weighted, axis=(1, 3)), jnp.sum(weighted * normed_g, axis=(1, 3))), "tile"
        )
        first = first / entry_count
        second = second / entry_count
        norm_back = rstd[:, None, :, None] * (
            weighted - first[:, None, :, None] - normed_g * second[:, None, :, None]
        )
        result = (
            seed_grad.astype(jnp.float32)
            + norm_back.reshape(frame_block, tile_rows, tile_cols, channels)
        ).astype(jnp.bfloat16)
        current = grads_out
        grads_out = jnp.where(is_valid, result, current)
        cache = jnp.where(is_valid, seed_rim[:2], cache)
        gain_acc = jnp.where(
            is_valid, gain_acc + jnp.sum(grad_hidden * normed, axis=(0, 1, 2)), gain_acc
        )
        bias_acc = jnp.where(is_valid, bias_acc + jnp.sum(grad_hidden, axis=(0, 1, 2)), bias_acc)
        act_cols = tap_columns(padded_active, frame_block, tile_rows, tile_cols, False)
        kernel_term = lax.dot_general(
            act_cols,
            seed_grad.reshape(-1, channels),
            (((0,), (0,)), ((), ())),
            preferred_element_type=jnp.float32,
        )
        store = jnp.where(is_valid, store + kernel_term, store)
        incoming = passed_along(result, "section", -1)
        return (incoming, cache, grads_out, store, gain_acc, bias_acc)

    loop_state = lax.fori_loop(
        0, tick_count, one_tick, (incoming, cache, grads_out, store, gain_acc, bias_acc)
    )
    incoming, cache, grads_out, store, gain_acc, bias_acc = loop_state
    kernel_shard = lax.psum_scatter(store, "tile", scatter_dimension=0, tiled=True)
    gain_sum, bias_sum = lax.psum((gain_acc, bias_acc), "tile")
    return (
        grads_out[None, :, None],
        (kernel_shard * scale)[None],
        (gain_sum * scale)[None],
        (bias_sum * scale)[None],
    )


def solution(mesh):
    in_specs = (
        P("section", None, "tile", None, None, None),
        P(None, "tile", None, None, None),
        P("section", None, None),
        P("section", None),
        P("section", None),
    )
    out_specs = (
        P("section", None, "tile", None, None, None),
        P("section", "tile", None),
        P("section", None),
        P("section", None),
    )
    return jax.shard_map(
        on_device, mesh=mesh, in_specs=in_specs, out_specs=out_specs, check_vma=False
    )
```

profile of v0, /device:TPU:1, one launch (start us, length us, event | category | flops | bytes accessed | tf_op | source)
XLA Modules:
  0.0 1797.8 jit_solution(10727232588783157938)
XLA Ops:
  2.0 205.9 %all-reduce.5 = (f32[8,32]{1,0:T(8,128)S(1)}, f32[8,32]{1,0:T(8,128)S(1)}) all-reduce(f32[8,32]{1,0:T(8,128)S(1)} %reduce_sum.98, f32[8,32]{1,0:T(8,128)S(1)} %reduce_sum.101), channel_id=1, replica_groups=mesh['section'=4,'tile'=64] {'tile'}, use_global_device_ids=true, to_apply=%region_5.6 | all-reduce | flops 512 | bytes 4096 | tf_op jit(solution)/shard_map/psum | solution.py:81
  211.6 11.8 collective-permute-start.6
  233.2 6.9 negate_exponential_fusion
  249.7 5.7 copy.37
  259.8 7.4 collective-permute-done.8
  270.5 1084.1 %while.27 = (s32[]{:T(128)}, bf16[8,4,8,256]{3,2,1,0:T(8,128)(2,1)S(1)}, bf16[2,6,10,256]{3,2,1,0:T(8,128)(2,1)}, bf16[8,4,8,256]{3,2,1,0:T(8,128)(2,1)}, f32[69...) while((s32[]{:T(128)}, ...), condition=%wide.region_13.14_spmd.clone, body=%wide.region_6.13_spmd.clone.sunk | while | flops 1824441856 | bytes 66399840 | solution.py:153
  276.1 6.1 add_select_fusion.5
  295.2 4.4 copy.48
  302.6 7.9 collective-permute-start.3
  323.6 203.6 %all-reduce.7 = (f32[8,32]{1,0:T(8,128)S(1)}, f32[8,32]{1,0:T(8,128)S(1)}) all-reduce(f32[8,32]{1,0:T(8,128)S(1)} %copy.51, f32[8,32]{1,0:T(8,128)S(1)} %copy.52), channel_id=1, replica_groups=mesh['section'=4,'tile'=64] {'tile'}, use_global_device_ids=true, to_apply=%region_10.10 | all-reduce | flops 512 | bytes 4096 | tf_op jit(solution)/shard_map/while/body/eval_jaxpr/psum | solution.py:123
  532.2 5.5 collective-permute-done.4
  537.8 10.4 collective-permute-start
  550.1 8.1 add_select_fusion.5
  578.6 7.9 collective-permute-start.3
  600.4 205.3 %all-reduce.7 = (f32[8,32]{1,0:T(8,128)S(1)}, f32[8,32]{1,0:T(8,128)S(1)}) all-reduce(f32[8,32]{1,0:T(8,128)S(1)} %copy.51, f32[8,32]{1,0:T(8,128)S(1)} %copy.52), channel_id=1, replica_groups=mesh['section'=4,'tile'=64] {'tile'}, use_global_device_ids=true, to_apply=%region_10.10 | all-reduce | flops 512 | bytes 4096 | tf_op jit(solution)/shard_map/while/body/eval_jaxpr/psum | solution.py:123
  820.1 8.1 add_select_fusion.5
  848.6 7.9 collective-permute-start.3
  870.3 205.2 %all-reduce.7 = (f32[8,32]{1,0:T(8,128)S(1)}, f32[8,32]{1,0:T(8,128)S(1)}) all-reduce(f32[8,32]{1,0:T(8,128)S(1)} %copy.51, f32[8,32]{1,0:T(8,128)S(1)} %copy.52), channel_id=1, replica_groups=mesh['section'=4,'tile'=64] {'tile'}, use_global_device_ids=true, to_apply=%region_10.10 | all-reduce | flops 512 | bytes 4096 | tf_op jit(solution)/shard_map/while/body/eval_jaxpr/psum | solution.py:123
  1090.0 8.1 add_select_fusion.5
  1118.5 7.9 collective-permute-start.3
  1140.2 205.6 %all-reduce.7 = (f32[8,32]{1,0:T(8,128)S(1)}, f32[8,32]{1,0:T(8,128)S(1)}) all-reduce(f32[8,32]{1,0:T(8,128)S(1)} %copy.51, f32[8,32]{1,0:T(8,128)S(1)} %copy.52), channel_id=1, replica_groups=mesh['section'=4,'tile'=64] {'tile'}, use_global_device_ids=true, to_apply=%region_10.10 | all-reduce | flops 512 | bytes 4096 | tf_op jit(solution)/shard_map/while/body/eval_jaxpr/psum | solution.py:123
  1354.6 8.5 copy.40
  1363.0 226.3 %fusion = f32[112,256]{1,0:T(8,128)S(1)} fusion(f32[6912,256]{1,0:T(8,128)} %copy.40), kind=kCustom, calls=%all-reduce-scatter | all-reduce-scatter fusion | flops 1835009 | bytes 7193600
  1592.6 200.9 %all-reduce.4 = (f32[256]{0:T(256)S(1)}, f32[256]{0:T(256)S(1)}) all-reduce(f32[256]{0:T(256)S(1)} %copy-done.7, f32[256]{0:T(256)S(1)} %copy-done.8), channel_id=1, replica_groups=mesh['section'=4,'tile'=64] {'tile'}, use_global_device_ids=true, to_apply=%region_15.16 | all-reduce | flops 512 | bytes 4096 | tf_op jit(solution)/shard_map/psum | solution.py:158
  (405 shorter events, 218.8 us)
Async XLA Ops:
  211.6 45.1 %collective-permute-start.6 = (bf16[8,4,1,256]{3,2,1,0:T(2,128)(2,1)S(1)}, bf16[8,4,1,256]{3,2,1,0:T(2,128)(2,1)S(1)}, u32[]{:S(2)}, u32[]{:S(2)}) collective-permute-start(bf16[8,4,1,256]{3,2,1,0:T(2,128)(2,1)S(1)} %get-tuple-element.844), channel_id=1, source_target_pairs={{1,0},{2,1},{3,2},{4,3},{5,4},{6,5},{7,6},{8,7},{9,8},{10,9},{11,1... | collective-permute-start | bytes 49160 | tf_op jit(solution)/shard_map/ppermute | solution.py:19
  223.3 33.4 %collective-permute-start.5 = (bf16[8,4,1,256]{3,2,1,0:T(2,128)(2,1)S(1)}, bf16[8,4,1,256]{3,2,1,0:T(2,128)(2,1)S(1)}, u32[]{:S(2)}, u32[]{:S(2)}) collective-permute-start(bf16[8,4,1,256]{3,2,1,0:T(2,128)(2,1)S(1)} %get-tuple-element.843), channel_id=1, source_target_pairs={{0,1},{1,2},{2,3},{3,4},{4,5},{5,6},{6,7},{7,8},{8,9},{9,10},{10,1... | collective-permute-start | bytes 49160 | tf_op jit(solution)/shard_map/ppermute | solution.py:19
  258.2 9.0 collective-permute-start.8
  270.5 30.6 %collective-permute-start = (bf16[8,4,1,256]{3,2,1,0:T(2,128)(2,1)S(1)}, bf16[8,4,1,256]{3,2,1,0:T(2,128)(2,1)S(1)}, u32[]{:S(2)}, u32[]{:S(2)}) collective-permute-start(bf16[8,4,1,256]{3,2,1,0:T(2,128)(2,1)S(1)} %get-tuple-element.1030), channel_id=1, source_target_pairs={{1,0},{2,1},{3,2},{4,3},{5,4},{6,5},{7,6},{8,7},{9,8},{10,9},{11,1... | collective-permute-start | bytes 49160 | tf_op jit(solution)/shard_map/while/body/eval_jaxpr/ppermute | solution.py:19
  274.0 27.1 %collective-permute-start.1 = (bf16[8,4,1,256]{3,2,1,0:T(2,128)(2,1)S(1)}, bf16[8,4,1,256]{3,2,1,0:T(2,128)(2,1)S(1)}, u32[]{:S(2)}, u32[]{:S(2)}) collective-permute-start(bf16[8,4,1,256]{3,2,1,0:T(2,128)(2,1)S(1)} %get-tuple-element.1031), channel_id=1, source_target_pairs={{0,1},{1,2},{2,3},{3,4},{4,5},{5,6},{6,7},{7,8},{8,9},{9,10},{10,1... | collective-permute-start | bytes 49160 | tf_op jit(solution)/shard_map/while/body/eval_jaxpr/ppermute | solution.py:19
  301.3 9.3 collective-permute-start.2
  302.6 9.5 collective-permute-start.3
  529.6 8.1 collective-permute-start.4
  537.8 39.4 %collective-permute-start = (bf16[8,4,1,256]{3,2,1,0:T(2,128)(2,1)S(1)}, bf16[8,4,1,256]{3,2,1,0:T(2,128)(2,1)S(1)}, u32[]{:S(2)}, u32[]{:S(2)}) collective-permute-start(bf16[8,4,1,256]{3,2,1,0:T(2,128)(2,1)S(1)} %get-tuple-element.1030), channel_id=1, source_target_pairs={{1,0},{2,1},{3,2},{4,3},{5,4},{6,5},{7,6},{8,7},{9,8},{10,9},{11,1... | collective-permute-start | bytes 49160 | tf_op jit(solution)/shard_map/while/body/eval_jaxpr/ppermute | solution.py:19
  548.2 29.0 %collective-permute-start.1 = (bf16[8,4,1,256]{3,2,1,0:T(2,128)(2,1)S(1)}, bf16[8,4,1,256]{3,2,1,0:T(2,128)(2,1)S(1)}, u32[]{:S(2)}, u32[]{:S(2)}) collective-permute-start(bf16[8,4,1,256]{3,2,1,0:T(2,128)(2,1)S(1)} %get-tuple-element.1031), channel_id=1, source_target_pairs={{0,1},{1,2},{2,3},{3,4},{4,5},{5,6},{6,7},{7,8},{8,9},{9,10},{10,1... | collective-permute-start | bytes 49160 | tf_op jit(solution)/shard_map/while/body/eval_jaxpr/ppermute | solution.py:19
  577.3 9.3 collective-permute-start.2
  578.6 9.2 collective-permute-start.3
  808.1 6.3 collective-permute-start.4
  814.5 32.6 %collective-permute-start = (bf16[8,4,1,256]{3,2,1,0:T(2,128)(2,1)S(1)}, bf16[8,4,1,256]{3,2,1,0:T(2,128)(2,1)S(1)}, u32[]{:S(2)}, u32[]{:S(2)}) collective-permute-start(bf16[8,4,1,256]{3,2,1,0:T(2,128)(2,1)S(1)} %get-tuple-element.1030), channel_id=1, source_target_pairs={{1,0},{2,1},{3,2},{4,3},{5,4},{6,5},{7,6},{8,7},{9,8},{10,9},{11,1... | collective-permute-start | bytes 49160 | tf_op jit(solution)/shard_map/while/body/eval_jaxpr/ppermute | solution.py:19
  817.9 29.3 %collective-permute-start.1 = (bf16[8,4,1,256]{3,2,1,0:T(2,128)(2,1)S(1)}, bf16[8,4,1,256]{3,2,1,0:T(2,128)(2,1)S(1)}, u32[]{:S(2)}, u32[]{:S(2)}) collective-permute-start(bf16[8,4,1,256]{3,2,1,0:T(2,128)(2,1)S(1)} %get-tuple-element.1031), channel_id=1, source_target_pairs={{0,1},{1,2},{2,3},{3,4},{4,5},{5,6},{6,7},{7,8},{8,9},{9,10},{10,1... | collective-permute-start | bytes 49160 | tf_op jit(solution)/shard_map/while/body/eval_jaxpr/ppermute | solution.py:19
  847.3 9.3 collective-permute-start.2
  848.6 9.2 collective-permute-start.3
  1084.4 32.6 %collective-permute-start = (bf16[8,4,1,256]{3,2,1,0:T(2,128)(2,1)S(1)}, bf16[8,4,1,256]{3,2,1,0:T(2,128)(2,1)S(1)}, u32[]{:S(2)}, u32[]{:S(2)}) collective-permute-start(bf16[8,4,1,256]{3,2,1,0:T(2,128)(2,1)S(1)} %get-tuple-element.1030), channel_id=1, source_target_pairs={{1,0},{2,1},{3,2},{4,3},{5,4},{6,5},{7,6},{8,7},{9,8},{10,9},{11,1... | collective-permute-start | bytes 49160 | tf_op jit(solution)/shard_map/while/body/eval_jaxpr/ppermute | solution.py:19
  1087.8 29.2 %collective-permute-start.1 = (bf16[8,4,1,256]{3,2,1,0:T(2,128)(2,1)S(1)}, bf16[8,4,1,256]{3,2,1,0:T(2,128)(2,1)S(1)}, u32[]{:S(2)}, u32[]{:S(2)}) collective-permute-start(bf16[8,4,1,256]{3,2,1,0:T(2,128)(2,1)S(1)} %get-tuple-element.1031), channel_id=1, source_target_pairs={{0,1},{1,2},{2,3},{3,4},{4,5},{5,6},{6,7},{7,8},{8,9},{9,10},{10,1... | collective-permute-start | bytes 49160 | tf_op jit(solution)/shard_map/while/body/eval_jaxpr/ppermute | solution.py:19
  1117.2 9.3 collective-permute-start.2
  1118.5 9.2 collective-permute-start.3
  1348.3 6.3 collective-permute-start.4
  1589.4 207.0 %collective-permute-start.10 = (f32[112,256]{1,0:T(8,128)S(1)}, f32[112,256]{1,0:T(8,128)S(1)}, u32[]{:S(2)}, u32[]{:S(2)}) collective-permute-start(f32[112,256]{1,0:T(8,128)S(1)} %fusion), channel_id=1, source_target_pairs={{0,2},{1,3},{2,4},{3,5},{4,6},{5,7},{6,8},{7,9},{8,10},{9,11},{10,... | collective-permute-start | bytes 344072
  1590.7 205.7 %collective-permute-start.9 = (f32[112,256]{1,0:T(8,128)S(1)}, f32[112,256]{1,0:T(8,128)S(1)}, u32[]{:S(2)}, u32[]{:S(2)}) collective-permute-start(f32[112,256]{1,0:T(8,128)S(1)} %fusion), channel_id=1, source_target_pairs={{0,1},{1,2},{2,3},{3,4},{4,5},{5,6},{6,7},{7,8},{8,9},{9,10},{10,1... | collective-permute-start | bytes 344072
  (26 other events, 520.0 us)
where the time goes:
time: 1810 us; the launch traced here: 1800 us
  blocking collectives  1450 us (80%)
  local copies, waits for them, and re-layouts  128 us (7%)
  starting transfers between devices  91.8 us (5%)
  other arithmetic  54.6 us (3%)
  matrix products  37.3 us (2%)
  waiting for transfers between devices  29.4 us (2%)
    psum x4, blocking collectives, one_tick(): lax.psum((jnp.sum(weighted, axis=(1, 3)), jnp.sum(weighted * normed_g, ax...  820 us
    unnamed x1, blocking collectives  226 us
    psum x1, blocking collectives, on_device(): lax.psum((jnp.sum(grouped, axis=(1, 3)), jnp.sum(grouped * grouped, axis=...  206 us
    psum x1, blocking collectives, on_device(): gain_sum, bias_sum = lax.psum((gain_acc, bias_acc), 'tile')  201 us
    ppermute x24, starting transfers between devices, passed_along(): lax.ppermute(value, axis, [(source, source + steps) for source in range(f...  87.3 us
    another operation x17, local copies, waits for them, and re-layouts  59.3 us
  transfers between devices with their start and end apart: 27, of which 10 were waited for; matrix products, arithmetic and copies ran while one was open for 8% of the time, Pallas kernels for 0%

commit v1 on v0

v1 whole, which is shorter than its diff:
```python
import functools
import math

import jax
import jax.numpy as jnp
from jax import lax
from jax.experimental import pallas as pl
from jax.experimental.pallas import tpu as pltpu
from jax.sharding import PartitionSpec as P

CH = 256
GROUPS = 32
PER_GROUP = CH // GROUPS
FR = 4
PX = 64
ROWS = FR * PX
ENTRIES = float(64 * 32 * PER_GROUP)
SCALE = 1.0 / math.sqrt(8 * 64 * 32)
EPS = 1e-05
MESH = pl.DeviceIdType.MESH
SIDES = ((-1, 0), (1, 0), (0, -1), (0, 1))
CORNERS = ((-1, -1), (-1, 1), (1, -1), (1, 1))
F32 = jnp.float32
BF16 = jnp.bfloat16


def kernel(
    x_ref, cot_ref, k_ref, gain_ref, bias_ref,
    out_ref, kout_ref, gout_ref, bout_ref,
    xr, cr, osend, orecv, rf, csend, hsend, nsend, gc, hr, nr, gp, gcol, kt_ref, a_t, xhat, dfac, stat,
    sa, sb, ua, ub, zg, zgr, dko, dks, dkr, dkb, rx, sx, ys, yr, sy, zs, zr, fs, fsend, frecv,
    ssem, zsem, hsem, nsem, gsem, tsem, pasem, pbsem, qasem, qbsem, csem, xsem, ysem, lsem,
):
    s = lax.axis_index("section")
    t = lax.axis_index("tile")
    x = t // 16
    zh = (t // 8) % 2
    y = (t // 2) % 4
    core = t % 2
    col = t % 8

    def dev(sec, x2, zh2, col2):
        return (sec, x2 * 16 + zh2 * 8 + col2)

    zpeer = dev(s, x, 1 - zh, col)
    cpeer = dev(s, x, zh, y * 2 + 1 - core)

    def remote(src, dst, sem_pair, device):
        return pltpu.make_async_remote_copy(
            src_ref=src, dst_ref=dst, send_sem=sem_pair.at[0], recv_sem=sem_pair.at[1],
            device_id=device, device_id_type=MESH,
        )

    xcopy = remote(x_ref.at[pl.ds((1 - zh) * FR, FR)], xr, zsem.at[0], zpeer)
    ccopy = remote(cot_ref.at[pl.ds((1 - zh) * FR, FR)], cr, zsem.at[1], zpeer)
    xcopy.start()

    @pl.when(s == 3)
    def _():
        ccopy.start()

    def patch(own, other):
        own = own.astype(F32)
        other = other.astype(F32)
        upper = jnp.where(zh == 0, own, other)
        lower = jnp.where(zh == 0, other, own)
        return jnp.concatenate([upper, lower], axis=1).reshape(ROWS, CH)

    lane = lax.broadcasted_iota(jnp.int32, (CH, 128), 1)
    chan = lax.broadcasted_iota(jnp.int32, (CH, 128), 0)
    gather_m = (chan // PER_GROUP == lane).astype(F32)
    lane2 = lax.broadcasted_iota(jnp.int32, (128, CH), 0)
    chan2 = lax.broadcasted_iota(jnp.int32, (128, CH), 1)
    spread_m = (chan2 // PER_GROUP == lane2).astype(F32)

    def grouped(first, second):
        return jnp.dot(
            jnp.concatenate([first, second], axis=0), gather_m,
            precision=lax.Precision.HIGHEST, preferred_element_type=F32,
        )

    def spread(groups):
        return jnp.dot(
            groups, spread_m, precision=lax.Precision.HIGHEST, preferred_element_type=F32
        )

    def col_copies(buf, sems):
        return [
            remote(buf.at[col], buf.at[col], sems.at[k - 1], dev(s, x, zh, (col + k) % 8))
            for k in range(1, 8)
        ]

    def x_copies(buf, sems):
        return [
            remote(buf.at[x], buf.at[x], sems.at[k - 1], dev(s, (x + k) % 4, zh, col))
            for k in range(1, 4)
        ]

    xcopy.wait()
    xv = patch(x_ref[pl.ds(zh * FR, FR)], xr[...])
    xhat[...] = xv
    x3 = xv.reshape(FR, PX, CH)
    sa[col] = jnp.concatenate(
        [grouped(jnp.sum(x3, axis=1), jnp.sum(x3 * x3, axis=1)), jnp.zeros((8, 128), F32)], axis=0
    )
    sa_copies = col_copies(sa, pasem)
    for c in sa_copies:
        c.start()

    def pack(value):
        rf[...] = value
        csend[...] = value.astype(BF16)
        v4 = value.reshape(FR, 8, 8, CH)
        hsend[0] = v4[:, 0].reshape(32, CH).astype(BF16)
        hsend[1] = v4[:, 7].reshape(32, CH).astype(BF16)
        for i, lead in ((2, 0), (3, 7)):
            for f in range(FR):
                rows = [rf[f * PX + r * 8 + lead : f * PX + r * 8 + lead + 1, :] for r in range(8)]
                stat[f * 8 : f * 8 + 8, :] = jnp.concatenate(rows, axis=0)
            hsend[i] = stat[...].astype(BF16)
        for i, pixel in enumerate((0, 7, 56, 63)):
            rows = [rf[f * PX + pixel : f * PX + pixel + 1, :] for f in range(FR)]
            nsend[i] = jnp.concatenate(rows + [jnp.zeros((12, CH), F32)], axis=0).astype(BF16)

    def rim_copies(sec):
        near, far = [], []
        for i, (dx, dc) in enumerate(SIDES):
            x2, c2 = (x + dx + 4) % 4, (col + dc + 8) % 8
            far.append(remote(hsend.at[i, pl.ds(0, 16)], hr.at[i, pl.ds(32, 16)], hsem.at[1, i], dev(sec, x2, 0, c2)))
            near.append(remote(hsend.at[i], hr.at[i, pl.ds(0, 32)], hsem.at[0, i], dev(sec, x2, zh, c2)))
        for i, (dx, dc) in enumerate(CORNERS):
            x2, c2 = (x + dx + 4) % 4, (col + dc + 8) % 8
            far.append(remote(nsend.at[i], nr.at[1, i], nsem.at[1, i], dev(sec, x2, 0, c2)))
            near.append(remote(nsend.at[i], nr.at[0, i], nsem.at[0, i], dev(sec, x2, zh, c2)))
        return near, far

    def center_copies(sec):
        near = remote(csend, gc.at[pl.ds(0, ROWS)], gsem.at[0], dev(sec, x, zh, col))
        far = remote(csend.at[pl.ds(0, 2 * PX)], gc.at[pl.ds(ROWS, 2 * PX)], gsem.at[1], dev(sec, x, 0, col))
        return near, far

    def send_patch(sec, remote_center):
        near, far = rim_copies(sec)
        center_near, center_far = center_copies(sec)

        @pl.when(zh == 1)
        def _():
            for c in far:
                c.start()
            center_far.start()

        for c in near:
            c.start()
        if remote_center:
            center_near.start()

    def wait_sent(sec, remote_center):
        near, far = rim_copies(sec)
        center_near, center_far = center_copies(sec)
        for c in near:
            c.wait_send()
        if remote_center:
            center_near.wait_send()

        @pl.when(zh == 1)
        def _():
            for c in far:
                c.wait_send()
            center_far.wait_send()

    @pl.when(s == 3)
    def _():
        ccopy.wait()
        value = patch(cot_ref[pl.ds(zh * FR, FR)], cr[...])
        pack(value)
        gc[0:ROWS, :] = value.astype(BF16)
        send_patch(3, False)

    def flip(i, carry):
        at = pl.multiple_of(i * CH, CH)
        kt_ref[pl.ds(at, CH), :] = jnp.transpose(k_ref[pl.ds(at, CH), :])
        return carry

    lax.fori_loop(0, 27, flip, 0)

    for c in sa_copies:
        c.wait()
    sb[x] = jnp.sum(sa[...], axis=0)
    sb_copies = x_copies(sb, pbsem)
    for c in sb_copies:
        c.start()
    for c in sb_copies:
        c.wait()
    total = spread(jnp.sum(sb[...], axis=0)[0:8] / ENTRIES)
    mean = total[0:4]
    rstd = lax.rsqrt(total[4:8] - mean * mean + EPS)
    gain = gain_ref[...]
    xh = (xhat[...].reshape(FR, PX, CH) - mean[:, None, :]) * rstd[:, None, :]
    h = xh * gain[None] + bias_ref[...][None]
    sg = jax.nn.sigmoid(h)
    xhat[...] = xh.reshape(ROWS, CH)
    dfac[...] = (sg * (1.0 + h * (1.0 - sg))).reshape(ROWS, CH)
    a_t[...] = jnp.transpose((h * sg).reshape(ROWS, CH)).astype(BF16)

    near, far = rim_copies(s)
    center_near, center_far = center_copies(s)

    @pl.when(s < 3)
    def _():
        center_near.wait_recv()

    for c in near:
        c.wait_recv()

    @pl.when(zh == 0)
    def _():
        for c in far:
            c.wait_recv()
        center_far.wait_recv()

    edge = (x > 0, x < 3, col > 0, col < 7)

    def fill(frames, row0, corner_set):
        sides = [hr[i, row0 : row0 + 8 * len(frames), :].astype(F32) for i in range(4)]
        top = jnp.where(edge[0], sides[1], 0.0)
        bottom = jnp.where(edge[1], sides[0], 0.0)
        left = jnp.where(edge[2], sides[3], 0.0)
        right = jnp.where(edge[3], sides[2], 0.0)
        corners = [nr[corner_set, i].astype(F32) for i in range(4)]
        top_left = jnp.where(edge[0] & edge[2], corners[3], 0.0)
        top_right = jnp.where(edge[0] & edge[3], corners[2], 0.0)
        bottom_left = jnp.where(edge[1] & edge[2], corners[1], 0.0)
        bottom_right = jnp.where(edge[1] & edge[3], corners[0], 0.0)
        for n, f in enumerate(frames):
            base = f * 10
            cell = slice(n * 8, n * 8 + 8)
            center = gc[f * PX : f * PX + PX, :].astype(F32).reshape(8, 8, CH)
            gp[base + 1 : base + 9, 8:16, :] = center
            gp[base, 8:16, :] = top[cell]
            gp[base + 9, 8:16, :] = bottom[cell]
            for r in range(8):
                gp[base + 1 + r, 7:8, :] = left[n * 8 + r : n * 8 + r + 1]
                gp[base + 1 + r, 16:17, :] = right[n * 8 + r : n * 8 + r + 1]
            gp[base, 7:8, :] = top_left[n : n + 1]
            gp[base, 16:17, :] = top_right[n : n + 1]
            gp[base + 9, 7:8, :] = bottom_left[n : n + 1]
            gp[base + 9, 16:17, :] = bottom_right[n : n + 1]
            for ox in range(3):
                strip = gp[base : base + 10, 7 + ox : 15 + ox, :]
                for oy in range(3):
                    tap = (2 - oy) * 3 + (2 - ox)
                    gcol[f * PX : f * PX + PX, tap * CH : tap * CH + CH] = (
                        strip[oy : oy + 8].reshape(PX, CH).astype(BF16)
                    )

    fill(range(4), 0, 0)

    @pl.when(zh == 0)
    def _():
        fill(range(4, 6), 32, 1)

    @pl.when(zh == 1)
    def _():
        gcol[ROWS:, :] = jnp.zeros((2 * PX, 9 * CH), BF16)

    da = jnp.zeros((ROWS, CH), F32)
    for kt in range(3):
        da = da + jnp.dot(
            gcol[(2 - kt) * PX : (2 - kt) * PX + ROWS, :],
            kt_ref[kt * 9 * CH : (kt + 1) * 9 * CH, :],
            preferred_element_type=F32,
        )
    dh = da * dfac[...]
    rf[...] = dh
    dh3 = dh.reshape(FR, PX, CH)
    dh_sum = jnp.sum(dh3, axis=1)
    dhx_sum = jnp.sum(dh3 * xhat[...].reshape(FR, PX, CH), axis=1)
    gain_part = jnp.sum(dhx_sum, axis=0, keepdims=True)
    bias_part = jnp.sum(dh_sum, axis=0, keepdims=True)
    ua[col] = jnp.concatenate(
        [
            grouped(dh_sum * gain, dhx_sum * gain),
            gain_part[:, :128], gain_part[:, 128:], bias_part[:, :128], bias_part[:, 128:],
            jnp.zeros((4, 128), F32),
        ],
        axis=0,
    )
    ua_copies = col_copies(ua, qasem)
    for c in ua_copies:
        c.start()

    def kernel_term(kt):
        def one(j, carry):
            rows = pl.multiple_of(kt * 9 * CH + j * CH, CH)
            lanes = pl.multiple_of(j * CH, CH)
            part = jnp.dot(
                a_t[...],
                gcol[(2 - kt) * PX : (2 - kt) * PX + ROWS, pl.ds(lanes, CH)],
                preferred_element_type=F32,
            )
            dko[pl.ds(rows, CH), :] = jnp.where(core == 0, part[:, :128], part[:, 128:])
            dks[pl.ds(rows, CH), :] = jnp.where(core == 0, part[:, 128:], part[:, :128]).astype(BF16)
            return carry

        lax.fori_loop(0, 9, one, 0)
        span = pl.ds(kt * 9 * CH, 9 * CH)
        copy = remote(dks.at[span], dkr.at[span], csem.at[kt], cpeer)
        copy.start()
        return copy

    core_copies = [kernel_term(0)]
    for c in ua_copies:
        c.wait()
    ub[x] = jnp.sum(ua[...], axis=0)
    ub_copies = x_copies(ub, qbsem)
    for c in ub_copies:
        c.start()
    core_copies.append(kernel_term(1))
    for c in ub_copies:
        c.wait()
    plane = jnp.sum(ub[...], axis=0)
    zg[...] = plane
    zg_copy = remote(zg, zgr, zsem.at[3], zpeer)
    zg_copy.start()
    both = spread(plane[0:8] / ENTRIES)
    xh = xhat[...].reshape(FR, PX, CH)
    u = rf[...].reshape(FR, PX, CH) * gain[None]
    dxn = rstd[:, None, :] * (u - both[0:4][:, None, :] - xh * both[4:8][:, None, :])
    result = gc[0:ROWS, :].astype(F32) + dxn.reshape(ROWS, CH)

    @pl.when(s == 3)
    def _():
        wait_sent(3, False)

    pack(result)

    @pl.when(s > 0)
    def _():
        send_patch(s - 1, True)

    final = csend[...].reshape(FR, 2, 32, CH)
    osend[...] = jnp.where(zh == 0, final[:, 1], final[:, 0])
    o_copy = remote(osend, orecv, zsem.at[2], zpeer)
    o_copy.start()
    out_ref[pl.ds(zh * FR, FR)] = jnp.where(zh == 0, final[:, 0], final[:, 1])

    core_copies.append(kernel_term(2))
    for kt, c in enumerate(core_copies):
        c.wait()

        def join(j, carry):
            rows = pl.multiple_of(kt * 9 * CH + j * CH, CH)
            both_cores = dko[pl.ds(rows, CH), :] + dkr[pl.ds(rows, CH), :].astype(F32)
            dko[pl.ds(rows, CH), :] = both_cores
            dkb[pl.ds(rows, CH), :] = both_cores.astype(BF16)
            return carry

        lax.fori_loop(0, 9, join, 0)

    rs_copies = []
    for k in range(1, 4):
        x2 = (x + k) % 4
        c = remote(
            dkb.at[pl.ds(pl.multiple_of(x2 * 1728, 16), 1728)], rx.at[x], xsem.at[k - 1], dev(s, x2, zh, col)
        )
        c.start()
        rs_copies.append(c)
    for c in rs_copies:
        c.wait()

    def add_x(i, carry):
        at = pl.multiple_of(i * 432, 16)
        acc = dko[pl.ds(pl.multiple_of(x * 1728 + i * 432, 16), 432), :]
        for k in range(1, 4):
            acc = acc + rx[(x + k) % 4, pl.ds(at, 432), :].astype(F32)
        sx[pl.ds(at, 432), :] = acc
        return carry

    lax.fori_loop(0, 4, add_x, 0)
    pad = jnp.zeros((8, 128), F32)
    for y2 in range(4):
        for z2 in range(2):
            at = z2 * 864 + y2 * 216
            ys[y2, z2] = jnp.concatenate([sx[at : at + 216, :], pad], axis=0).astype(BF16)
    y_copies = []
    for k in range(1, 4):
        y2 = (y + k) % 4
        c = remote(ys.at[y2], yr.at[y], ysem.at[k - 1], dev(s, x, zh, y2 * 2 + core))
        c.start()
        y_copies.append(c)
    for c in y_copies:
        c.wait()
    for z2 in range(2):
        acc = sx[pl.ds(pl.multiple_of(z2 * 864 + y * 216, 8), 216), :]
        for k in range(1, 4):
            acc = acc + yr[(y + k) % 4, z2].astype(F32)[0:216]
        sy[z2] = acc
    zs[...] = jnp.concatenate([sy[1 - zh], pad], axis=0).astype(BF16)
    z_copy = remote(zs, zr, lsem.at[0], zpeer)
    z_copy.start()
    z_copy.wait()
    fs[...] = sy[zh] + zr[...].astype(F32)[0:216]
    low = fs[0:108, :]
    high = fs[108:216, :]
    mine = jnp.where(core == 0, low, high)
    fsend[0:108, :] = jnp.where(core == 0, high, low)
    fsend[108:112, :] = jnp.zeros((4, 128), F32)
    f_copy = remote(fsend, frecv, lsem.at[1], cpeer)
    f_copy.start()
    f_copy.wait()
    theirs = frecv[0:108, :]
    kout_ref[:, 0:128] = jnp.where(core == 0, mine, theirs) * SCALE
    kout_ref[:, 128:256] = jnp.where(core == 0, theirs, mine) * SCALE

    zg_copy.wait()
    sums = (zg[...] + zgr[...]) * SCALE
    gout_ref[:, 0:128] = sums[8:9]
    gout_ref[:, 128:256] = sums[9:10]
    bout_ref[:, 0:128] = sums[10:11]
    bout_ref[:, 128:256] = sums[11:12]
    o_copy.wait()
    out_ref[pl.ds((1 - zh) * FR, FR)] = orecv[...]

    @pl.when(s > 0)
    def _():
        wait_sent(s - 1, True)


def on_device(saved_inputs, cotangent, kernels, gains, biases):
    inputs = saved_inputs.reshape(8, 32, CH)
    seeds = cotangent.reshape(8, 32, CH)
    vmem = pl.BlockSpec(memory_space=pltpu.VMEM)
    v = pltpu.VMEM
    dma = pltpu.SemaphoreType.DMA
    out, kout, gout, bout = pl.pallas_call(
        kernel,
        out_shape=(
            jax.ShapeDtypeStruct((8, 32, CH), BF16),
            jax.ShapeDtypeStruct((108, CH), F32),
            jax.ShapeDtypeStruct((1, CH), F32),
            jax.ShapeDtypeStruct((1, CH), F32),
        ),
        in_specs=[vmem] * 5,
        out_specs=[vmem] * 4,
        scratch_shapes=[
            v((FR, 32, CH), BF16), v((FR, 32, CH), BF16), v((FR, 32, CH), BF16), v((FR, 32, CH), BF16),
            v((ROWS, CH), F32), v((ROWS, CH), BF16), v((4, 32, CH), BF16), v((4, 16, CH), BF16),
            v((ROWS + 2 * PX, CH), BF16), v((4, 48, CH), BF16), v((2, 4, 16, CH), BF16),
            v((60, 24, CH), F32), v((ROWS + 2 * PX, 9 * CH), BF16), v((27 * CH, CH), BF16),
            v((CH, ROWS), BF16), v((ROWS, CH), F32), v((ROWS, CH), F32), v((32, CH), F32),
            v((8, 16, 128), F32), v((4, 16, 128), F32), v((8, 16, 128), F32), v((4, 16, 128), F32),
            v((16, 128), F32), v((16, 128), F32),
            v((27 * CH, 128), F32), v((27 * CH, 128), BF16), v((27 * CH, 128), BF16), v((27 * CH, 128), BF16),
            v((4, 1728, 128), BF16), v((1728, 128), F32), v((4, 2, 224, 128), BF16), v((4, 2, 224, 128), BF16),
            v((2, 216, 128), F32), v((224, 128), BF16), v((224, 128), BF16), v((216, 128), F32),
            v((112, 128), F32), v((112, 128), F32),
            dma((1,)), dma((4, 2)), dma((2, 4, 2)), dma((2, 4, 2)), dma((2, 2)), dma((1,)),
            dma((7, 2)), dma((3, 2)), dma((7, 2)), dma((3, 2)), dma((3, 2)), dma((3, 2)), dma((3, 2)), dma((2, 2)),
        ],
        compiler_params=pltpu.CompilerParams(has_side_effects=True, vmem_limit_bytes=52 * 2**20),
        name="blocks",
    )(inputs, seeds, kernels[0], gains, biases)
    return (
        out.reshape(1, 8, 1, 4, 8, CH),
        kout[None],
        gout,
        bout,
    )


def solution(mesh):
    in_specs = (
        P("section", None, "tile", None, None, None),
        P(None, "tile", None, None, None),
        P("section", None, None),
        P("section", None),
        P("section", None),
    )
    out_specs = (
        P("section", None, "tile", None, None, None),
        P("section", "tile", None),
        P("section", None),
        P("section", None),
    )
    return jax.shard_map(
        on_device, mesh=mesh, in_specs=in_specs, out_specs=out_specs, check_vma=False
    )
```

time: 1810 us -> 139 us (0.08)
  blocking collectives: 1450 us -> 0 us
  Pallas kernels: 0 us -> 132 us
  local copies, waits for them, and re-layouts: 128 us -> 5.7 us
  starting transfers between devices: 91.8 us -> 0 us
  other arithmetic: 54.6 us -> 0 us
  matrix products: 37.3 us -> 0 us
  waiting for transfers between devices: 29.4 us -> 0 us
    psum x6 -> x0, blocking collectives: 1230 us -> none  [the longest x4 820 us: one_tick(): lax.psum((jnp.sum(weighted, axis=(1, 3)), jnp.sum(weighted * normed_g, ax...]
    unnamed x1 -> x0, blocking collectives: 226 us -> none
    pallas_call x0 -> x1, Pallas kernels: none -> 132 us  [on_device(): pl.pallas_call(kernel, out_shape=(jax.ShapeDtypeStruct((8, 32, CH), BF16)...]
    ppermute x24 -> x0, starting transfers between devices: 87.3 us -> none  [passed_along(): lax.ppermute(value, axis, [(source, source + steps) for source in range(f...]
    another operation x18 -> x0, local copies, waits for them, and re-layouts: 65.1 us -> none
    dot_general x8 -> x0, matrix products: 37.3 us -> none  [the longest x4 30.5 us: one_tick(): lax.dot_general(act_cols, seed_grad.reshape(-1, channels), (((0,), (0,)),...]
    ppermute x24 -> x0, waiting for transfers between devices: 28.9 us -> none  [passed_along(): lax.ppermute(value, axis, [(source, source + steps) for source in range(f...]
    while x141 -> x0, local copies, waits for them, and re-layouts: 20.9 us -> none
  transfers between devices with their start and end apart: 27 -> 0, of which waited for: 10 -> 0; matrix products, arithmetic and copies ran while one was open for 8% -> 0% of each run, Pallas kernels for 0% -> 0%
where the time goes in v1:
time: 139 us
  Pallas kernels  132 us (95%)
  local copies, waits for them, and re-layouts  5.7 us (4%)
    pallas_call x1, Pallas kernels, on_device(): pl.pallas_call(kernel, out_shape=(jax.ShapeDtypeStruct((8, 32, CH), BF16)...  132 us
    unnamed x12, local copies, waits for them, and re-layouts  5.7 us

profile of v1, /device:TPU:1, one launch (start us, length us, event | category | flops | bytes accessed | tf_op | source)
XLA Modules:
  0.0 138.7 jit_solution(2584842243177399226)
XLA Ops:
  0.6 0.0 copy-start
  0.6 0.9 copy-done
  1.5 0.0 copy-start.1
  1.5 0.9 copy-done.1
  2.4 0.0 copy-start.2
  2.4 0.7 copy-done.2
  3.1 0.0 copy-start.3
  3.1 0.7 copy-done.3
  3.8 132.3 %blocks.1 = (bf16[8,32,256]{2,1,0:T(8,128)(2,1)S(1)}, f32[108,256]{1,0:T(8,128)S(1)}, f32[1,256]{1,0:T(1,128)S(1)}, f32[1,256]{1,0:T(1,128)S(1)}) custom-call(bf16[8,32,256]{2,1,0:T(8,128)(2,1)S(1)} %bitcast.7, bf16[8,32,256]{2,1,0:T(8,128)(2,1)S(1)} %bitcast.8, bf16[6912,256]{1,0:T(8,128)(2,1)} %bitcast.11, f32[1,256]{1,0:T(1,128)S(1)} %copy-done.2, ...), custom_call_target="tpu_custom_call" | custom-call | tf_op jit(solution)/shard_map/blocks/pallas_call | solution.py:435
  136.1 0.8 copy.10
  136.9 0.7 copy.14
  137.5 0.6 copy.15
  138.1 0.6 copy.16
Async XLA Ops:
  0.6 0.9 copy-start
  1.5 0.9 copy-start.1
  2.4 0.7 copy-start.2
  3.1 0.7 copy-start.3

commit v2 on v1

v2 whole, which is shorter than its diff:
```python
import functools
import math

import jax
import jax.numpy as jnp
from jax import lax
from jax.experimental import pallas as pl
from jax.experimental.pallas import tpu as pltpu
from jax.sharding import PartitionSpec as P

CH = 256
GROUPS = 32
PER_GROUP = CH // GROUPS
FR = 4
PX = 64
ROWS = FR * PX
ALL = ROWS + 2 * PX
ENTRIES = float(64 * 32 * PER_GROUP)
SCALE = 1.0 / math.sqrt(8 * 64 * 32)
EPS = 1e-05
VMEM_LIMIT = 63 * 2**20
MESH = pl.DeviceIdType.MESH
SIDES = ((-1, 0), (1, 0), (0, -1), (0, 1))
CORNERS = ((-1, -1), (-1, 1), (1, -1), (1, 1))
AROUND = [(dx, dy, dc) for dx in (-1, 0, 1) for dy, dc in ((0, 0), (-1, 1), (0, 1), (1, 1))]
CHIPS = [(dx, dy) for dx in range(4) for dy in range(4)]
QUARTERS = ((0, 7), (7, 14), (14, 21), (21, 27))
F32 = jnp.float32
BF16 = jnp.bfloat16


def kernel(
    x_hbm, cot_hbm, k_hbm, gain_hbm, bias_hbm,
    out_ref, kout_ref, gout_ref, bout_ref,
    x_ref, cot_ref, k_ref, gain_ref, bias_ref,
    xr, cr, osend, orecv, rf, strip,
    wc, wh, wn, gc, gh, gn, xwc, xwh, xwn, xgc, xgh, xgn,
    xc, xs, xn, gp, gcen, gcol, ccol, kt_ref, a_t, xhat, dfac, da,
    sa, sb, ua, ub, unear, ufar, xt, xtr, mom, zg, zgr,
    dko, dks, dkr, b0, b1, rx, ry, p0, p1, r2,
    lsem, zsem, wgs, whs, wns, xgs, xhs, xns, acs, aps, ucs, ups, tsem, csem, xsem, ysem, psem,
):
    s = lax.axis_index("section")
    t = lax.axis_index("tile")
    x = t // 16
    zh = (t // 8) % 2
    y = (t // 2) % 4
    core = t % 2
    col = t % 8
    chip = x * 4 + y

    def at(sec, dx, z2, dy, dc):
        return (sec, ((x + dx + 4) % 4) * 16 + z2 * 8 + ((y + dy + 4) % 4) * 2 + (core + dc) % 2)

    def beside(sec, dx, z2, dcol):
        return (sec, ((x + dx + 4) % 4) * 16 + z2 * 8 + (col + dcol + 8) % 8)

    zpeer = at(s, 0, 1 - zh, 0, 0)
    cpeer = at(s, 0, zh, 0, 1)

    def remote(src, dst, pair, device):
        return pltpu.make_async_remote_copy(
            src_ref=src, dst_ref=dst, send_sem=pair.at[0], recv_sem=pair.at[1],
            device_id=device, device_id_type=MESH,
        )

    x_load = pltpu.make_async_copy(x_hbm, x_ref, lsem.at[0])
    cot_load = pltpu.make_async_copy(cot_hbm, cot_ref, lsem.at[1])
    k_load = pltpu.make_async_copy(k_hbm, k_ref, lsem.at[2])
    gain_load = pltpu.make_async_copy(gain_hbm, gain_ref, lsem.at[3])
    bias_load = pltpu.make_async_copy(bias_hbm, bias_ref, lsem.at[4])
    x_load.start()
    gain_load.start()
    bias_load.start()

    @pl.when(s == 3)
    def _():
        cot_load.start()

    k_load.start()

    barrier = pltpu.get_barrier_semaphore()

    def greet(device):
        pl.semaphore_signal(barrier, inc=1, device_id=device, device_id_type=MESH)

    plane = {(dx, 0, dy, 0) for dx, dy in CHIPS}
    plane |= {(0, z, dy, dc) for z in range(2) for dy in range(4) for dc in range(2)}
    plane |= {(dx, z, 0, dc) for z in range(2) for dx in range(4) for dc in range(2)}
    plane = sorted(plane - {(0, 0, 0, 0)})
    for dx, z, dy, dc in plane:
        greet(at(s, dx, (zh + z) % 2, dy, dc))

    @pl.when(s < 3)
    def _():
        for dx, dy, dc in AROUND:
            greet(at(s + 1, dx, zh, dy, dc))

        @pl.when(zh == 0)
        def _():
            for dx, dy, dc in AROUND:
                greet(at(s + 1, dx, 1, dy, dc))

    @pl.when(s == 3)
    def _():
        for dx, dy, dc in AROUND:
            if (dx, dy, dc) != (0, 0, 0):
                greet(at(3, dx, zh, dy, dc))

        @pl.when(zh == 0)
        def _():
            for dx, dy, dc in AROUND:
                greet(at(3, dx, 1, dy, dc))

    expected = len(plane) + jnp.where(s > 0, (1 + zh) * len(AROUND), 0)
    expected = expected + jnp.where(s == 3, len(AROUND) - 1 + zh * len(AROUND), 0)
    pl.semaphore_wait(barrier, expected)

    theirs = pl.ds((1 - zh) * FR, FR)
    ours = pl.ds(zh * FR, FR)
    x_copy = remote(x_hbm.at[theirs], xr, zsem.at[0], zpeer)
    cot_copy = remote(cot_hbm.at[theirs], cr, zsem.at[1], zpeer)

    @pl.when(s == 3)
    def _():
        cot_copy.start()

    x_copy.start()

    def patch(own, other):
        own = own.astype(F32)
        other = other.astype(F32)
        upper = jnp.where(zh == 0, own, other)
        lower = jnp.where(zh == 0, other, own)
        return jnp.concatenate([upper, lower], axis=1).reshape(ROWS, CH)

    def indicator(shape, channel_dim):
        channel = lax.broadcasted_iota(jnp.int32, shape, channel_dim)
        group = lax.broadcasted_iota(jnp.int32, shape, 1 - channel_dim)
        return (channel // PER_GROUP == group).astype(F32)

    def grouped(first, second):
        return jnp.dot(
            jnp.concatenate([first, second], axis=0), indicator((CH, 128), 0),
            precision=lax.Precision.HIGHEST, preferred_element_type=F32,
        )

    def spread(groups):
        return jnp.dot(
            groups, indicator((128, CH), 1), precision=lax.Precision.HIGHEST, preferred_element_type=F32
        )

    def core_sum_copy(buf, pair):
        return remote(buf.at[core], buf.at[core], pair, cpeer)

    def chip_copies(buf, sems):
        return [
            remote(buf.at[chip], buf.at[chip], sems.at[i], at(s, dx, zh, dy, 0))
            for i, (dx, dy) in enumerate(CHIPS) if i
        ]

    def pack(value, center, sides, corners):
        rf[...] = value
        center[...] = value.astype(BF16)
        v4 = value.reshape(FR, 8, 8, CH)
        sides[0] = v4[:, 0].reshape(32, CH).astype(BF16)
        sides[1] = v4[:, 7].reshape(32, CH).astype(BF16)
        for i, lead in ((2, 0), (3, 7)):
            for f in range(FR):
                rows = [rf[f * PX + r * 8 + lead : f * PX + r * 8 + lead + 1, :] for r in range(8)]
                strip[f * 8 : f * 8 + 8, :] = jnp.concatenate(rows, axis=0)
            sides[i] = strip[...].astype(BF16)
        for i, pixel in enumerate((0, 7, 56, 63)):
            rows = [rf[f * PX + pixel : f * PX + pixel + 1, :] for f in range(FR)]
            corners[i] = jnp.concatenate(rows + [jnp.zeros((12, CH), F32)], axis=0).astype(BF16)

    def piece_copies(sec, send, recv, sems):
        center, sides, corners = send
        center_r, sides_r, corners_r = recv
        gs, hs, ns = sems
        near, far = [], []
        for i, (dx, dc) in enumerate(CORNERS):
            near.append(remote(corners.at[i], corners_r.at[0, i], ns.at[0, i], beside(sec, dx, zh, dc)))
            far.append(remote(corners.at[i], corners_r.at[1, i], ns.at[1, i], beside(sec, dx, 0, dc)))
        for i, (dx, dc) in enumerate(SIDES):
            near.append(remote(sides.at[i], sides_r.at[i, pl.ds(0, 32)], hs.at[0, i], beside(sec, dx, zh, dc)))
            far.append(
                remote(sides.at[i, pl.ds(0, 16)], sides_r.at[i, pl.ds(32, 16)], hs.at[1, i], beside(sec, dx, 0, dc))
            )
        middle = remote(center, center_r.at[pl.ds(0, ROWS)], gs.at[0], beside(sec, 0, zh, 0))
        far.append(
            remote(center.at[pl.ds(0, 2 * PX)], center_r.at[pl.ds(ROWS, 2 * PX)], gs.at[1], beside(sec, 0, 0, 0))
        )
        return near, middle, far

    def each(copies, what):
        for c in copies:
            getattr(c, what)()

    def send_pieces(copies, with_middle):
        near, middle, far = copies
        each(near, "start")
        if with_middle:
            middle.start()

        @pl.when(zh == 1)
        def _():
            each(far, "start")

    def wait_sent(copies, with_middle):
        near, middle, far = copies
        each(near + ([middle] if with_middle else []), "wait_send")

        @pl.when(zh == 1)
        def _():
            each(far, "wait_send")

    def wait_received(copies, with_middle):
        near, middle, far = copies
        each(near + ([middle] if with_middle else []), "wait_recv")

        @pl.when(zh == 0)
        def _():
            each(far, "wait_recv")

    w_send, w_recv, w_sems = (wc, wh, wn), (gc, gh, gn), (wgs, whs, wns)
    x_send, x_recv, x_sems = (xwc, xwh, xwn), (xgc, xgh, xgn), (xgs, xhs, xns)

    @pl.when(s == 3)
    def _():
        cot_load.wait()
        cot_copy.wait()
        value = patch(cot_ref[ours], cr[...])
        pack(value, wc, wh, wn)
        gc[0:ROWS, :] = value.astype(BF16)
        send_pieces(piece_copies(3, w_send, w_recv, w_sems), False)

    x_load.wait()
    x_copy.wait()
    xv = patch(x_ref[ours], xr[...])
    xhat[...] = xv
    x3 = xv.reshape(FR, PX, CH)
    sa[core] = grouped(jnp.sum(x3, axis=1), jnp.sum(x3 * x3, axis=1))
    sa_copy = core_sum_copy(sa, acs)
    sa_copy.start()

    @pl.when(s > 0)
    def _():
        pack(xv, xwc, xwh, xwn)

    sa_copy.wait()
    sb[chip] = sa[0] + sa[1]
    sb_copies = chip_copies(sb, aps)
    each(sb_copies, "start")

    @pl.when(s > 0)
    def _():
        send_pieces(piece_copies(s - 1, x_send, x_recv, x_sems), True)

    k_load.wait()

    def flip(i, carry):
        rows = pl.ds(pl.multiple_of(i * CH, CH), CH)
        kt_ref[rows, :] = jnp.transpose(k_ref[rows, :])
        return carry

    lax.fori_loop(0, 27, flip, 0)

    gain_load.wait()
    bias_load.wait()
    each(sb_copies, "wait")
    xt[...] = jnp.sum(sb[...], axis=0)
    xt_near = remote(xt, xtr.at[0], tsem.at[0], at(s - 1, 0, zh, 0, 0))
    xt_far = remote(xt, xtr.at[1], tsem.at[1], at(s - 1, 0, 0, 0, 0))

    @pl.when(s > 0)
    def _():
        xt_near.start()

        @pl.when(zh == 1)
        def _():
            xt_far.start()

    def moments(total):
        total = spread(total / ENTRIES)
        mean = total[0:4]
        return mean, lax.rsqrt(total[4:8] - mean * mean + EPS)

    mean, rstd = moments(xt[...])
    gain = gain_ref[...]
    xh = (xhat[...].reshape(FR, PX, CH) - mean[:, None, :]) * rstd[:, None, :]
    h = xh * gain[None] + bias_ref[...][None]
    sg = jax.nn.sigmoid(h)
    xhat[...] = xh.reshape(ROWS, CH)
    dfac[...] = (sg * (1.0 + h * (1.0 - sg))).reshape(ROWS, CH)
    a_t[...] = jnp.transpose((h * sg).reshape(ROWS, CH)).astype(BF16)

    @pl.when(s < 3)
    def _():
        wait_received(piece_copies(s, x_send, x_recv, x_sems), True)
        remote(xt, xtr.at[0], tsem.at[0], cpeer).wait_recv()

        @pl.when(zh == 0)
        def _():
            remote(xt, xtr.at[1], tsem.at[1], cpeer).wait_recv()

        def normalise(frames, part, row0):
            mean_up, rstd_up = moments(xtr[part])
            n = len(frames)
            mom[frames[0] : frames[0] + n, :] = rstd_up[0:n]
            m, r = mean_up[0:n][:, None, :], rstd_up[0:n][:, None, :]
            px = slice(frames[0] * PX, (frames[0] + n) * PX)
            xc[px, :] = ((xgc[px, :].astype(F32).reshape(n, PX, CH) - m) * r).reshape(n * PX, CH)
            for i in range(4):
                side = xgh[i, row0 : row0 + 8 * n, :].astype(F32).reshape(n, 8, CH)
                xs[i, row0 : row0 + 8 * n, :] = ((side - m) * r).reshape(8 * n, CH)
                xn[part, i, 0:n, :] = (xgn[part, i].astype(F32)[0:n] - mean_up[0:n]) * rstd_up[0:n]

        normalise(range(4), 0, 0)

        @pl.when(zh == 0)
        def _():
            normalise(range(4, 6), 1, 32)

    arriving = piece_copies(s, w_send, w_recv, w_sems)

    edge = (x > 0, x < 3, col > 0, col < 7)

    def columns(frames, center, sides, corners, out):
        top = jnp.where(edge[0], sides[1], 0.0)
        bottom = jnp.where(edge[1], sides[0], 0.0)
        left = jnp.where(edge[2], sides[3], 0.0)
        right = jnp.where(edge[3], sides[2], 0.0)
        top_left = jnp.where(edge[0] & edge[2], corners[3], 0.0)
        top_right = jnp.where(edge[0] & edge[3], corners[2], 0.0)
        bottom_left = jnp.where(edge[1] & edge[2], corners[1], 0.0)
        bottom_right = jnp.where(edge[1] & edge[3], corners[0], 0.0)
        center = center.reshape(len(frames), 8, 8, CH)
        for i, f in enumerate(frames):
            base = f * 10
            cell = slice(i * 8, i * 8 + 8)
            gp[base + 1 : base + 9, 8:16, :] = center[i]
            gp[base, 8:16, :] = top[cell]
            gp[base + 9, 8:16, :] = bottom[cell]
            for r in range(8):
                gp[base + 1 + r, 7:8, :] = left[i * 8 + r : i * 8 + r + 1]
                gp[base + 1 + r, 16:17, :] = right[i * 8 + r : i * 8 + r + 1]
            gp[base, 7:8, :] = top_left[i : i + 1]
            gp[base, 16:17, :] = top_right[i : i + 1]
            gp[base + 9, 7:8, :] = bottom_left[i : i + 1]
            gp[base + 9, 16:17, :] = bottom_right[i : i + 1]
            for ox in range(3):
                band = gp[base : base + 10, 7 + ox : 15 + ox, :]
                for oy in range(3):
                    tap = (2 - oy) * 3 + (2 - ox)
                    out[f * PX : f * PX + PX, tap * CH : tap * CH + CH] = (
                        band[oy : oy + 8].reshape(PX, CH).astype(BF16)
                    )

    def fill(frames, part, row0):
        n = len(frames)
        px = slice(frames[0] * PX, (frames[0] + n) * PX)
        columns(
            frames, gc[px, :].astype(F32),
            [gh[i, row0 : row0 + 8 * n, :].astype(F32) for i in range(4)],
            [gn[part, i].astype(F32)[0:n] for i in range(4)], gcol,
        )

    def fill_correction(frames, part, row0, sums):
        n = len(frames)
        both = spread(sums / ENTRIES)
        r_up = mom[frames[0] : frames[0] + n, :]
        c1, c2 = r_up * both[0:n], r_up * both[4 : 4 + n]

        def term(hat, rows):
            value = c1[:, None, :] + hat.reshape(n, rows, CH) * c2[:, None, :]
            return value.reshape(n * rows, CH)

        px = slice(frames[0] * PX, (frames[0] + n) * PX)
        center = term(xc[px, :], PX)
        if part == 0:
            gcen[...] = gc[px, :].astype(F32) - center
        columns(
            frames, center, [term(xs[i, row0 : row0 + 8 * n, :], 8) for i in range(4)],
            [c1 + xn[part, i, 0:n, :] * c2 for i in range(4)], ccol,
        )

    def convolve(cols):
        value = jnp.zeros((ROWS, CH), F32)
        for kt in range(3):
            value = value + jnp.dot(
                cols[(2 - kt) * PX : (2 - kt) * PX + ROWS, :],
                kt_ref[kt * 9 * CH : (kt + 1) * 9 * CH, :],
                preferred_element_type=F32,
            )
        return value

    near, middle, far = arriving
    each(near, "wait_recv")

    @pl.when(s < 3)
    def _():
        middle.wait_recv()

    fill(range(4), 0, 0)

    @pl.when(zh == 0)
    def _():
        each(far, "wait_recv")
        fill(range(4, 6), 1, 32)

    @pl.when(zh == 1)
    def _():
        gcol[ROWS:, :] = jnp.zeros((2 * PX, 9 * CH), BF16)
        ccol[ROWS:, :] = jnp.zeros((2 * PX, 9 * CH), BF16)

    da[...] = convolve(gcol)

    @pl.when(s == 3)
    def _():
        gcen[...] = gc[0:ROWS, :].astype(F32)
        ccol[...] = jnp.zeros_like(ccol)

    @pl.when(s < 3)
    def _():
        remote(zg.at[pl.ds(0, 8)], unear, tsem.at[3], cpeer).wait_recv()
        fill_correction(range(4), 0, 0, unear[...])

        @pl.when(zh == 0)
        def _():
            remote(zg.at[pl.ds(0, 8)], ufar, tsem.at[2], cpeer).wait_recv()
            fill_correction(range(4, 6), 1, 32, ufar[...])

        da[...] = da[...] - convolve(ccol)

    dh3 = (da[...] * dfac[...]).reshape(FR, PX, CH)
    dh_sum = jnp.sum(dh3, axis=1)
    dhx_sum = jnp.sum(dh3 * xhat[...].reshape(FR, PX, CH), axis=1)
    gain_part = jnp.sum(dhx_sum, axis=0, keepdims=True)
    bias_part = jnp.sum(dh_sum, axis=0, keepdims=True)
    ua[core] = jnp.concatenate(
        [
            grouped(dh_sum * gain, dhx_sum * gain),
            gain_part[:, :128], gain_part[:, 128:], bias_part[:, :128], bias_part[:, 128:],
            jnp.zeros((4, 128), F32),
        ],
        axis=0,
    )
    ua_copy = core_sum_copy(ua, ucs)
    ua_copy.start()

    w = gcen[...] + (rstd[:, None, :] * (dh3 * gain[None])).reshape(ROWS, CH)
    dfac[...] = w

    @pl.when(s == 3)
    def _():
        wait_sent(piece_copies(3, w_send, w_recv, w_sems), False)

    w_copies = piece_copies(s - 1, w_send, w_recv, w_sems)

    @pl.when(s > 0)
    def _():
        pack(w, wc, wh, wn)
        each(w_copies[0], "start")
        w_copies[1].start()

    ua_copy.wait()
    ub[chip] = ua[0] + ua[1]
    ub_copies = chip_copies(ub, ups)
    each(ub_copies, "start")

    @pl.when((s > 0) & (zh == 1))
    def _():
        each(w_copies[2], "start")

    def quarter(q):
        first, last = QUARTERS[q]

        def one(tap, carry):
            rows = pl.multiple_of(tap * CH, CH)
            lanes = pl.multiple_of((tap % 9) * CH, CH)
            frames = pl.multiple_of((2 - tap // 9) * PX, PX)
            part = jnp.dot(
                a_t[...], gcol[pl.ds(frames, ROWS), pl.ds(lanes, CH)], preferred_element_type=F32
            ) - jnp.dot(
                a_t[...], ccol[pl.ds(frames, ROWS), pl.ds(lanes, CH)], preferred_element_type=F32
            )
            dko[pl.ds(rows, CH), :] = jnp.where(core == 0, part[:, :128], part[:, 128:])
            dks[pl.ds(rows, CH), :] = jnp.where(core == 0, part[:, 128:], part[:, :128]).astype(BF16)
            return carry

        lax.fori_loop(first, last, one, 0)
        span = pl.ds(q * 1728, 1728)
        copy = remote(dks.at[span], dkr.at[span], csem.at[q], cpeer)
        copy.start()
        return copy

    pad8 = jnp.zeros((8, 128), F32)
    y_copies = []

    def x_first(q):
        return pltpu.make_async_remote_copy(
            src_ref=b0.at[q], dst_ref=rx.at[x], send_sem=xsem.at[q, 0], recv_sem=xsem.at[x, 1],
            device_id=at(s, q - x, zh, 0, 0), device_id_type=MESH,
        )

    def x_first_arrival(source):
        return pltpu.make_async_remote_copy(
            src_ref=b0.at[0], dst_ref=rx.at[source], send_sem=xsem.at[0, 0], recv_sem=xsem.at[source, 1],
            device_id=cpeer, device_id_type=MESH,
        )

    def join(q, copy):
        copy.wait()
        for half in range(4):
            at0 = q * 1728 + half * 432
            both_cores = dko[at0 : at0 + 432, :] + dkr[at0 : at0 + 432, :].astype(F32)
            dko[at0 : at0 + 432, :] = both_cores
            if half < 2:
                b0[q, half * 432 : half * 432 + 432, :] = both_cores.astype(BF16)
            else:
                for i in range(2):
                    piece = jnp.concatenate([both_cores[i * 216 : i * 216 + 216], pad8], axis=0)
                    b1[q, (half - 2) * 2 + i] = piece.astype(BF16)

        @pl.when(x != q)
        def _():
            x_first(q).start()

        for k in range(1, 4):
            y2 = (y + k) % 4
            c = remote(b1.at[q, y2], ry.at[y, q], ysem.at[q, k - 1], at(s, 0, zh, k, 0))
            c.start()
            y_copies.append(c)

    core_copies = [quarter(0), quarter(1)]
    each(ub_copies, "wait")
    total = jnp.sum(ub[...], axis=0)
    zg[...] = total
    near_sum = remote(zg.at[pl.ds(0, 8)], unear, tsem.at[3], at(s - 1, 0, zh, 0, 0))
    far_sum = remote(zg.at[pl.ds(0, 8)], ufar, tsem.at[2], at(s - 1, 0, 0, 0, 0))

    @pl.when(s > 0)
    def _():
        near_sum.start()

        @pl.when(zh == 1)
        def _():
            far_sum.start()

    join(0, core_copies[0])
    zg_copy = remote(zg, zgr, zsem.at[3], zpeer)
    zg_copy.start()
    both = spread(total[0:8] / ENTRIES)
    c1, c2 = rstd * both[0:4], rstd * both[4:8]
    xh = xhat[...].reshape(FR, PX, CH)
    final = dfac[...].reshape(FR, PX, CH) - c1[:, None, :] - xh * c2[:, None, :]
    final = final.astype(BF16).reshape(FR, 2, 32, CH)
    osend[...] = jnp.where(zh == 0, final[:, 1], final[:, 0])
    o_copy = remote(osend, orecv, zsem.at[2], zpeer)
    o_copy.start()
    out_ref[ours] = jnp.where(zh == 0, final[:, 0], final[:, 1])

    core_copies.append(quarter(2))
    join(1, core_copies[1])
    core_copies.append(quarter(3))
    join(2, core_copies[2])
    join(3, core_copies[3])

    pad4 = jnp.zeros((4, 128), F32)

    def cut(value, buf, i):
        buf[i, 0] = jnp.concatenate([value[0:108], pad4], axis=0).astype(BF16)
        buf[i, 1] = jnp.concatenate([value[108:216], pad4], axis=0).astype(BF16)

    each(y_copies, "wait")
    for q in range(4):
        acc = dko[pl.ds(pl.multiple_of(q * 1728 + 864 + y * 216, 8), 216), :]
        for k in range(1, 4):
            acc = acc + ry[(y + k) % 4, q].astype(F32)[0:216]
        cut(acc, p1, q)

    def to_owner(plane_id, i, dc):
        dx, dy = (i, 0) if plane_id else (0, i)
        index = (x + i) % 4 if plane_id else (y + i) % 4
        slot = x if plane_id else y
        buf = p1 if plane_id else p0
        return pltpu.make_async_remote_copy(
            src_ref=buf.at[index, (core + dc) % 2], dst_ref=r2.at[core, zh, slot],
            send_sem=psem.at[plane_id, 0, i * 2 + dc], recv_sem=psem.at[zh, 1, i * 2 + dc],
            device_id=at(s, dx, plane_id, dy, dc), device_id_type=MESH,
        )

    def deliver(plane_id):
        for i in range(4):
            for dc in range(2):
                if (i, dc) != (0, 0):
                    to_owner(plane_id, i, dc).start()

        @pl.when(zh != plane_id)
        def _():
            to_owner(plane_id, 0, 0).start()

        @pl.when(zh == plane_id)
        def _():
            buf, slot = (p1, x) if plane_id else (p0, y)
            r2[core, zh, slot] = buf[slot, core]

    deliver(1)
    for k in range(1, 4):
        x_first_arrival((x + k) % 4).wait_recv()
    for half in range(2):
        acc = dko[pl.ds(pl.multiple_of(x * 1728 + half * 432, 16), 432), :]
        for k in range(1, 4):
            acc = acc + rx[(x + k) % 4, half * 432 : half * 432 + 432, :].astype(F32)
        cut(acc[0:216], p0, half * 2)
        cut(acc[216:432], p0, half * 2 + 1)
    deliver(0)

    zg_copy.wait()
    sums = (zg[...] + zgr[...]) * SCALE
    gout_ref[:, 0:128] = sums[8:9]
    gout_ref[:, 128:256] = sums[9:10]
    bout_ref[:, 0:128] = sums[10:11]
    bout_ref[:, 128:256] = sums[11:12]
    o_copy.wait()
    out_ref[theirs] = orecv[...]

    @pl.when(s > 0)
    def _():
        wait_sent(piece_copies(s - 1, x_send, x_recv, x_sems), True)
        wait_sent(w_copies, True)
        xt_near.wait_send()
        near_sum.wait_send()

        @pl.when(zh == 1)
        def _():
            xt_far.wait_send()
            far_sum.wait_send()

    for q in range(4):

        @pl.when(x != q)
        def _():
            x_first(q).wait_send()

    for source in range(2):
        for j in range(8):
            arrival = pltpu.make_async_remote_copy(
                src_ref=p0.at[0, 0], dst_ref=r2.at[0, 0, 0], send_sem=psem.at[0, 0, j],
                recv_sem=psem.at[source, 1, j], device_id=cpeer, device_id_type=MESH,
            )
            if j:
                arrival.wait_recv()
            else:

                @pl.when(zh != source)
                def _():
                    arrival.wait_recv()

    for half in range(2):
        acc = jnp.zeros((112, 128), F32)
        for source in range(2):
            for i in range(4):
                acc = acc + r2[half, source, i].astype(F32)
        kout_ref[:, half * 128 : half * 128 + 128] = acc[0:108] * SCALE

    for plane_id in range(2):
        for i in range(4):
            for dc in range(2):
                if (i, dc) != (0, 0):
                    to_owner(plane_id, i, dc).wait_send()
                else:

                    @pl.when(zh != plane_id)
                    def _():
                        to_owner(plane_id, 0, 0).wait_send()


def on_device(saved_inputs, cotangent, kernels, gains, biases):
    inputs = saved_inputs.reshape(8, 32, CH)
    seeds = cotangent.reshape(8, 32, CH)
    vmem = pl.BlockSpec(memory_space=pltpu.VMEM)
    hbm = pl.BlockSpec(memory_space=pltpu.HBM)
    v = pltpu.VMEM
    dma = pltpu.SemaphoreType.DMA
    out, kout, gout, bout = pl.pallas_call(
        kernel,
        out_shape=(
            jax.ShapeDtypeStruct((8, 32, CH), BF16),
            jax.ShapeDtypeStruct((108, CH), F32),
            jax.ShapeDtypeStruct((1, CH), F32),
            jax.ShapeDtypeStruct((1, CH), F32),
        ),
        in_specs=[hbm] * 5,
        out_specs=[vmem] * 4,
        scratch_shapes=[
            v((8, 32, CH), BF16), v((8, 32, CH), BF16), v((27 * CH, CH), BF16), v((1, CH), F32), v((1, CH), F32),
            v((FR, 32, CH), BF16), v((FR, 32, CH), BF16), v((FR, 32, CH), BF16), v((FR, 32, CH), BF16),
            v((ROWS, CH), F32), v((32, CH), F32),
            v((ROWS, CH), BF16), v((4, 32, CH), BF16), v((4, 16, CH), BF16),
            v((ALL, CH), BF16), v((4, 48, CH), BF16), v((2, 4, 16, CH), BF16),
            v((ROWS, CH), BF16), v((4, 32, CH), BF16), v((4, 16, CH), BF16),
            v((ALL, CH), BF16), v((4, 48, CH), BF16), v((2, 4, 16, CH), BF16),
            v((ALL, CH), F32), v((4, 48, CH), F32), v((2, 4, 16, CH), F32), v((60, 24, CH), F32),
            v((ROWS, CH), F32), v((ALL, 9 * CH), BF16), v((ALL, 9 * CH), BF16), v((27 * CH, CH), BF16),
            v((CH, ROWS), BF16), v((ROWS, CH), F32), v((ROWS, CH), F32), v((ROWS, CH), F32),
            v((2, 8, 128), F32), v((16, 8, 128), F32), v((2, 16, 128), F32), v((16, 16, 128), F32),
            v((8, 128), F32), v((8, 128), F32), v((8, 128), F32), v((2, 8, 128), F32), v((8, CH), F32),
            v((16, 128), F32), v((16, 128), F32),
            v((27 * CH, 128), F32), v((27 * CH, 128), BF16), v((27 * CH, 128), BF16),
            v((4, 864, 128), BF16), v((4, 4, 224, 128), BF16), v((4, 864, 128), BF16), v((4, 4, 224, 128), BF16),
            v((4, 2, 112, 128), BF16), v((4, 2, 112, 128), BF16), v((2, 2, 4, 112, 128), BF16),
            dma((5,)), dma((4, 2)), dma((2, 2)), dma((2, 4, 2)), dma((2, 4, 2)),
            dma((2, 2)), dma((2, 4, 2)), dma((2, 4, 2)),
            dma((2,)), dma((16, 2)), dma((2,)), dma((16, 2)), dma((4, 2)), dma((4, 2)),
            dma((4, 2)), dma((4, 3, 2)), dma((2, 2, 8)),
        ],
        compiler_params=pltpu.CompilerParams(
            collective_id=0, has_side_effects=True, vmem_limit_bytes=VMEM_LIMIT
        ),
        name="blocks",
    )(inputs, seeds, kernels[0], gains, biases)
    return out.reshape(1, 8, 1, 4, 8, CH), kout[None], gout, bout


def solution(mesh):
    in_specs = (
        P("section", None, "tile", None, None, None),
        P(None, "tile", None, None, None),
        P("section", None, None),
        P("section", None),
        P("section", None),
    )
    out_specs = (
        P("section", None, "tile", None, None, None),
        P("section", "tile", None),
        P("section", None),
        P("section", None),
    )
    return jax.shard_map(
        on_device, mesh=mesh, in_specs=in_specs, out_specs=out_specs, check_vma=False
    )
```

time: 139 us -> 107 us (0.77)
  the two profiles are of different devices: /device:TPU:1 before, /device:TPU:6 now
where the time goes in v2:
time: 107 us
  Pallas kernels  101 us (94%)
  local copies, waits for them, and re-layouts  5.68 us (5%)
    pallas_call x1, Pallas kernels, on_device(): pl.pallas_call(kernel, out_shape=(jax.ShapeDtypeStruct((8, 32, CH), BF16)...  101 us
    unnamed x4, local copies, waits for them, and re-layouts  5.68 us

profile of v2, /device:TPU:6, one launch (start us, length us, event | category | flops | bytes accessed | tf_op | source)
XLA Modules:
  0.0 107.2 jit_solution(4252163974243096184)
XLA Ops:
  0.6 100.9 %blocks.1 = (bf16[8,32,256]{2,1,0:T(8,128)(2,1)}, f32[108,256]{1,0:T(8,128)}, f32[1,256]{1,0:T(1,128)}, f32[1,256]{1,0:T(1,128)}) custom-call(bf16[8,32,256]{2,1,0:T(8,128)(2,1)} %bitcast.8, bf16[8,32,256]{2,1,0:T(8,128)(2,1)} %bitcast.9, bf16[6912,256]{1,0:T(8,128)(2,1)} %bitcast.7, f32[1,256]{1,0:T(1,128)} %gain_hbm.1, f32[1,256]{1,0:T(1,128)} %bias_hbm.1), custom_call_target="tpu_custom_call" | custom-call | tf_op jit(solution)/shard_map/blocks/pallas_call | solution.py:687
  101.5 1.7 %copy.10 = f32[1,108,256]{2,0,1:T(1,128)} copy(f32[1,108,256]{2,1,0:T(8,128)} %bitcast.11) | data formatting | bytes 221184
  103.2 1.6 %copy.14 = bf16[1,8,1,4,8,256]{5,4,3,2,1,0:T(8,128)(2,1)} copy(bf16[1,8,1,4,8,256]{5,4,3,2,1,0:T(8,128)(2,1)} %bitcast.10) | data formatting | bytes 262144
  104.8 1.2 %copy.15 = f32[1,256]{1,0:T(1,128)} copy(f32[1,256]{1,0:T(1,128)} %get-tuple-element.22) | data formatting | bytes 2048
  106.0 1.2 %copy.16 = f32[1,256]{1,0:T(1,128)} copy(f32[1,256]{1,0:T(1,128)} %get-tuple-element.23) | data formatting | bytes 2048

commit v3 on v2

--- a/solution.py
+++ b/solution.py
@@ -24,7 +24,7 @@
 CORNERS = ((-1, -1), (-1, 1), (1, -1), (1, 1))
 AROUND = [(dx, dy, dc) for dx in (-1, 0, 1) for dy, dc in ((0, 0), (-1, 1), (0, 1), (1, 1))]
 CHIPS = [(dx, dy) for dx in range(4) for dy in range(4)]
-QUARTERS = ((0, 7), (7, 14), (14, 21), (21, 27))
+QUARTER = 1728
 F32 = jnp.float32
 BF16 = jnp.bfloat16
 
@@ -33,12 +33,12 @@
     x_hbm, cot_hbm, k_hbm, gain_hbm, bias_hbm,
     out_ref, kout_ref, gout_ref, bout_ref,
     x_ref, cot_ref, k_ref, gain_ref, bias_ref,
-    xr, cr, osend, orecv, rf, strip,
+    xr, xst, xstr, osend, orecv, rf, strip, lrs, rows_s, nooks, lr,
     wc, wh, wn, gc, gh, gn, xwc, xwh, xwn, xgc, xgh, xgn,
     xc, xs, xn, gp, gcen, gcol, ccol, kt_ref, a_t, xhat, dfac, da,
     sa, sb, ua, ub, unear, ufar, xt, xtr, mom, zg, zgr,
-    dko, dks, dkr, b0, b1, rx, ry, p0, p1, r2,
-    lsem, zsem, wgs, whs, wns, xgs, xhs, xns, acs, aps, ucs, ups, tsem, csem, xsem, ysem, psem,
+    dko, dks, dkr, b0, b1, rx, ry, p0, p1, t0, t1, r2x, r2y, p3, r3,
+    lsem, zsem, dsem, wgs, whs, wns, xgs, xhs, xns, acs, aps, ucs, ups, tsem, csem, xsem, ysem, xsem2, ysem2, psem,
 ):
     s = lax.axis_index("section")
     t = lax.axis_index("tile")
@@ -84,10 +84,8 @@
     def greet(device):
         pl.semaphore_signal(barrier, inc=1, device_id=device, device_id_type=MESH)
 
-    plane = {(dx, 0, dy, 0) for dx, dy in CHIPS}
-    plane |= {(0, z, dy, dc) for z in range(2) for dy in range(4) for dc in range(2)}
-    plane |= {(dx, z, 0, dc) for z in range(2) for dx in range(4) for dc in range(2)}
-    plane = sorted(plane - {(0, 0, 0, 0)})
+    plane = [(dx, 0, dy, 0) for dx, dy in CHIPS if (dx, dy) != (0, 0)]
+    plane += [(0, 1, 0, 0), (0, 1, 0, 1), (0, 0, 0, 1)]
     for dx, z, dy, dc in plane:
         greet(at(s, dx, (zh + z) % 2, dy, dc))
 
@@ -106,26 +104,15 @@
         for dx, dy, dc in AROUND:
             if (dx, dy, dc) != (0, 0, 0):
                 greet(at(3, dx, zh, dy, dc))
-
-        @pl.when(zh == 0)
-        def _():
-            for dx, dy, dc in AROUND:
-                greet(at(3, dx, 1, dy, dc))
+            greet(at(3, dx, 1 - zh, dy, dc))
 
     expected = len(plane) + jnp.where(s > 0, (1 + zh) * len(AROUND), 0)
-    expected = expected + jnp.where(s == 3, len(AROUND) - 1 + zh * len(AROUND), 0)
+    expected = expected + jnp.where(s == 3, 2 * len(AROUND) - 1, 0)
     pl.semaphore_wait(barrier, expected)
 
     theirs = pl.ds((1 - zh) * FR, FR)
     ours = pl.ds(zh * FR, FR)
     x_copy = remote(x_hbm.at[theirs], xr, zsem.at[0], zpeer)
-    cot_copy = remote(cot_hbm.at[theirs], cr, zsem.at[1], zpeer)
-
-    @pl.when(s == 3)
-    def _():
-        cot_copy.start()
-
-    x_copy.start()
 
     def patch(own, other):
         own = own.astype(F32)
@@ -159,9 +146,20 @@
             for i, (dx, dy) in enumerate(CHIPS) if i
         ]
 
+    x_load.wait()
+
+    def tile_sums(frames):
+        value = x_ref[frames].astype(F32)
+        return grouped(jnp.sum(value, axis=1), jnp.sum(value * value, axis=1))
+
+    xst[...] = tile_sums(theirs)
+    xst_copy = remote(xst, xstr, zsem.at[1], zpeer)
+    xst_copy.start()
+    own_sums = tile_sums(ours)
+
     def pack(value, center, sides, corners):
         rf[...] = value
-        center[...] = value.astype(BF16)
+        center[...] = value.astype(BF16).reshape(FR, 2, 32, CH)
         v4 = value.reshape(FR, 8, 8, CH)
         sides[0] = v4[:, 0].reshape(32, CH).astype(BF16)
         sides[1] = v4[:, 7].reshape(32, CH).astype(BF16)
@@ -180,16 +178,16 @@
         gs, hs, ns = sems
         near, far = [], []
         for i, (dx, dc) in enumerate(CORNERS):
-            near.append(remote(corners.at[i], corners_r.at[0, i], ns.at[0, i], beside(sec, dx, zh, dc)))
-            far.append(remote(corners.at[i], corners_r.at[1, i], ns.at[1, i], beside(sec, dx, 0, dc)))
+            near.append(remote(corners.at[i], corners_r.at[i, 0], ns.at[0, i], beside(sec, dx, zh, dc)))
+            far.append(remote(corners.at[i], corners_r.at[i, 1], ns.at[1, i], beside(sec, dx, 0, dc)))
         for i, (dx, dc) in enumerate(SIDES):
             near.append(remote(sides.at[i], sides_r.at[i, pl.ds(0, 32)], hs.at[0, i], beside(sec, dx, zh, dc)))
             far.append(
                 remote(sides.at[i, pl.ds(0, 16)], sides_r.at[i, pl.ds(32, 16)], hs.at[1, i], beside(sec, dx, 0, dc))
             )
-        middle = remote(center, center_r.at[pl.ds(0, ROWS)], gs.at[0], beside(sec, 0, zh, 0))
+        middle = remote(center, center_r.at[pl.ds(0, FR)], gs.at[0], beside(sec, 0, zh, 0))
         far.append(
-            remote(center.at[pl.ds(0, 2 * PX)], center_r.at[pl.ds(ROWS, 2 * PX)], gs.at[1], beside(sec, 0, 0, 0))
+            remote(center.at[pl.ds(0, 2)], center_r.at[pl.ds(FR, 2)], gs.at[1], beside(sec, 0, 0, 0))
         )
         return near, middle, far
 
@@ -226,36 +224,122 @@
     w_send, w_recv, w_sems = (wc, wh, wn), (gc, gh, gn), (wgs, whs, wns)
     x_send, x_recv, x_sems = (xwc, xwh, xwn), (xgc, xgh, xgn), (xgs, xhs, xns)
 
+    frames_of = (pl.ds(0, 6), pl.ds(4, 4))
+    count_of = (6, 4)
+
+    def direct_copies(plane_id):
+        n = count_of[plane_id]
+        lead = 4 * plane_id
+        lr_rows = pl.ds(16 * plane_id, 32 - 16 * plane_id)
+        row_rows = pl.ds(8 * lead, 8 * n)
+        down = 2 * zh - 1
+        pair = dsem.at[plane_id]
+
+        def send(src, dst, slot, device):
+            return pltpu.make_async_remote_copy(
+                src_ref=src, dst_ref=dst, send_sem=pair.at[0, slot], recv_sem=dsem.at[zh, 1, slot],
+                device_id=device, device_id_type=MESH,
+            )
+
+        nook_rows = pl.ds(plane_id, 2 - plane_id)
+        landing = pl.ds(0, 2 - plane_id)
+        copies = [
+            send(nooks.at[0, nook_rows], gn.at[2 * zh, landing], 3, beside(3, down, plane_id, -1)),
+            send(nooks.at[1, nook_rows], gn.at[2 * zh + 1, landing], 4, beside(3, down, plane_id, 1)),
+            send(rows_s.at[row_rows], gh.at[zh, pl.ds(0, 8 * n)], 2, beside(3, down, plane_id, 0)),
+            send(lrs.at[0, lr_rows], lr.at[0, zh, pl.ds(0, 32 - 16 * plane_id)], 0, beside(3, 0, plane_id, -1)),
+            send(lrs.at[1, lr_rows], lr.at[1, zh, pl.ds(0, 32 - 16 * plane_id)], 1, beside(3, 0, plane_id, 1)),
+        ]
+        center = send(
+            cot_hbm.at[frames_of[plane_id]], gc.at[pl.ds(0, n), zh], 5, beside(3, 0, plane_id, 0)
+        )
+        return copies, center
+
+    def own_half(plane_id):
+        return pltpu.make_async_copy(
+            cot_hbm.at[frames_of[plane_id]], gc.at[pl.ds(0, count_of[plane_id]), plane_id], lsem.at[5]
+        )
+
+    def direct_arrivals(plane_id):
+        n = count_of[plane_id]
+        arrivals = []
+        for source in range(2):
+            sizes = (
+                lr.at[0, 0, pl.ds(0, 32 - 16 * plane_id)], lr.at[0, 0, pl.ds(0, 32 - 16 * plane_id)],
+                gh.at[0, pl.ds(0, 8 * n)],
+                gn.at[0, pl.ds(0, 2 - plane_id)], gn.at[0, pl.ds(0, 2 - plane_id)],
+            ) + ((gc.at[pl.ds(0, n), 0],) if source != plane_id else ())
+            for slot, ref in enumerate(sizes):
+                arrivals.append(
+                    pltpu.make_async_remote_copy(
+                        src_ref=ref, dst_ref=ref, send_sem=dsem.at[0, 0, slot],
+                        recv_sem=dsem.at[source, 1, slot], device_id=cpeer, device_id_type=MESH,
+                    )
+                )
+        return arrivals
+
     @pl.when(s == 3)
     def _():
+        for plane_id in range(2):
+
+            @pl.when(zh == plane_id)
+            def _():
+                direct_copies(1 - plane_id)[1].start()
+                own_half(plane_id).start()
+
         cot_load.wait()
-        cot_copy.wait()
-        value = patch(cot_ref[ours], cr[...])
-        pack(value, wc, wh, wn)
-        gc[0:ROWS, :] = value.astype(BF16)
-        send_pieces(piece_copies(3, w_send, w_recv, w_sems), False)
-
-    x_load.wait()
-    x_copy.wait()
-    xv = patch(x_ref[ours], xr[...])
-    xhat[...] = xv
-    x3 = xv.reshape(FR, PX, CH)
-    sa[core] = grouped(jnp.sum(x3, axis=1), jnp.sum(x3 * x3, axis=1))
+        rf[...] = cot_ref[...].astype(F32).reshape(ROWS, CH)
+        for i, lead in ((0, 0), (1, 7)):
+            for f in range(8):
+                picks = [rf[f * 32 + r * 8 + lead : f * 32 + r * 8 + lead + 1, :] for r in range(4)]
+                strip[f * 4 : f * 4 + 4, :] = jnp.concatenate(picks, axis=0)
+            lrs[i] = strip[...].astype(BF16)
+        outer_rows = []
+        for f in range(8):
+            outer_rows.append(
+                jnp.where(zh == 0, rf[f * 32 : f * 32 + 8, :], rf[f * 32 + 24 : f * 32 + 32, :])
+            )
+        rows_s[...] = jnp.concatenate(outer_rows, axis=0).astype(BF16)
+        for i, end in ((0, 0), (1, 7)):
+            for part in range(2):
+                picks = [outer_rows[part * 4 + f][end : end + 1] for f in range(4)]
+                nooks[i, part] = jnp.concatenate(picks + [jnp.zeros((12, CH), F32)], axis=0).astype(BF16)
+        for plane_id in (1, 0):
+            each(direct_copies(plane_id)[0], "start")
+        x_copy.start()
+
+    def direct_done():
+        for plane_id in range(2):
+
+            @pl.when(zh == plane_id)
+            def _():
+                each(direct_arrivals(plane_id), "wait_recv")
+                own_half(plane_id).wait()
+                n = count_of[plane_id]
+                for i in range(2):
+                    halves = [lr[i, z2].astype(F32)[0 : 4 * n].reshape(n, 4, CH) for z2 in range(2)]
+                    gh[2 + i, 0 : 8 * n, :] = (
+                        jnp.concatenate(halves, axis=1).reshape(8 * n, CH).astype(BF16)
+                    )
+
+            each(direct_copies(plane_id)[0], "wait_send")
+
+            @pl.when(zh != plane_id)
+            def _():
+                direct_copies(plane_id)[1].wait_send()
+
+    xst_copy.wait()
+    sa[core] = own_sums + xstr[...]
     sa_copy = core_sum_copy(sa, acs)
     sa_copy.start()
-
-    @pl.when(s > 0)
-    def _():
-        pack(xv, xwc, xwh, xwn)
-
     sa_copy.wait()
     sb[chip] = sa[0] + sa[1]
     sb_copies = chip_copies(sb, aps)
     each(sb_copies, "start")
 
-    @pl.when(s > 0)
-    def _():
-        send_pieces(piece_copies(s - 1, x_send, x_recv, x_sems), True)
+    @pl.when(s < 3)
+    def _():
+        x_copy.start()
 
     k_load.wait()
 
@@ -265,6 +349,15 @@
         return carry
 
     lax.fori_loop(0, 27, flip, 0)
+
+    x_copy.wait()
+    xv = patch(x_ref[ours], xr[...])
+    xhat[...] = xv
+
+    @pl.when(s > 0)
+    def _():
+        pack(xv, xwc, xwh, xwn)
+        send_pieces(piece_copies(s - 1, x_send, x_recv, x_sems), True)
 
     gain_load.wait()
     bias_load.wait()
@@ -310,11 +403,12 @@
             mom[frames[0] : frames[0] + n, :] = rstd_up[0:n]
             m, r = mean_up[0:n][:, None, :], rstd_up[0:n][:, None, :]
             px = slice(frames[0] * PX, (frames[0] + n) * PX)
-            xc[px, :] = ((xgc[px, :].astype(F32).reshape(n, PX, CH) - m) * r).reshape(n * PX, CH)
+            up = xgc[frames[0] : frames[0] + n].astype(F32).reshape(n, PX, CH)
+            xc[px, :] = ((up - m) * r).reshape(n * PX, CH)
             for i in range(4):
                 side = xgh[i, row0 : row0 + 8 * n, :].astype(F32).reshape(n, 8, CH)
                 xs[i, row0 : row0 + 8 * n, :] = ((side - m) * r).reshape(8 * n, CH)
-                xn[part, i, 0:n, :] = (xgn[part, i].astype(F32)[0:n] - mean_up[0:n]) * rstd_up[0:n]
+                xn[part, i, 0:n, :] = (xgn[i, part].astype(F32)[0:n] - mean_up[0:n]) * rstd_up[0:n]
 
         normalise(range(4), 0, 0)
 
@@ -359,11 +453,10 @@
 
     def fill(frames, part, row0):
         n = len(frames)
-        px = slice(frames[0] * PX, (frames[0] + n) * PX)
         columns(
-            frames, gc[px, :].astype(F32),
+            frames, gc[frames[0] : frames[0] + n].astype(F32),
             [gh[i, row0 : row0 + 8 * n, :].astype(F32) for i in range(4)],
-            [gn[part, i].astype(F32)[0:n] for i in range(4)], gcol,
+            [gn[i, part].astype(F32)[0:n] for i in range(4)], gcol,
         )
 
     def fill_correction(frames, part, row0, sums):
@@ -379,7 +472,7 @@
         px = slice(frames[0] * PX, (frames[0] + n) * PX)
         center = term(xc[px, :], PX)
         if part == 0:
-            gcen[...] = gc[px, :].astype(F32) - center
+            gcen[...] = gc[0:FR].astype(F32).reshape(ROWS, CH) - center
         columns(
             frames, center, [term(xs[i, row0 : row0 + 8 * n, :], 8) for i in range(4)],
             [c1 + xn[part, i, 0:n, :] * c2 for i in range(4)], ccol,
@@ -396,17 +489,24 @@
         return value
 
     near, middle, far = arriving
-    each(near, "wait_recv")
+
+    @pl.when(s == 3)
+    def _():
+        direct_done()
 
     @pl.when(s < 3)
     def _():
+        each(near, "wait_recv")
         middle.wait_recv()
 
     fill(range(4), 0, 0)
 
     @pl.when(zh == 0)
     def _():
-        each(far, "wait_recv")
+        @pl.when(s < 3)
+        def _():
+            each(far, "wait_recv")
+
         fill(range(4, 6), 1, 32)
 
     @pl.when(zh == 1)
@@ -414,11 +514,106 @@
         gcol[ROWS:, :] = jnp.zeros((2 * PX, 9 * CH), BF16)
         ccol[ROWS:, :] = jnp.zeros((2 * PX, 9 * CH), BF16)
 
+    def taps(first, last):
+        def one(tap, carry):
+            rows = pl.multiple_of(tap * CH, CH)
+            lanes = pl.multiple_of((tap % 9) * CH, CH)
+            frames = pl.multiple_of((2 - tap // 9) * PX, PX)
+            part = jnp.dot(
+                a_t[...], gcol[pl.ds(frames, ROWS), pl.ds(lanes, CH)], preferred_element_type=F32
+            ) - jnp.dot(
+                a_t[...], ccol[pl.ds(frames, ROWS), pl.ds(lanes, CH)], preferred_element_type=F32
+            )
+            dko[pl.ds(rows, CH), :] = jnp.where(core == 0, part[:, :128], part[:, 128:])
+            dks[pl.ds(rows, CH), :] = jnp.where(core == 0, part[:, 128:], part[:, :128]).astype(BF16)
+            return carry
+
+        lax.fori_loop(first, last, one, 0)
+
+    def own_rows(step, offset, count):
+        q = (x + 1 + step) % 4
+        return pl.ds(pl.multiple_of(q * QUARTER + offset, 8), count)
+
+    def core_copy(step):
+        q = (x + 1 + step) % 4
+        span = pl.ds(pl.multiple_of(q * QUARTER, 16), QUARTER)
+        return remote(dks.at[span], dkr.at[span], csem.at[step], cpeer)
+
+    def quarter(step):
+        q = (x + 1 + step) % 4
+        if step == 0:
+            @pl.when(x < 3)
+            def _():
+                taps(7 * x + 6, 7 * x + 7)
+
+        if step < 3:
+            taps(7 * q, 7 * q + 7 - q // 3)
+        else:
+            taps(7 * x, 7 * x + 6)
+        core_copy(step).start()
+
+    def x_first(step):
+        return remote(b0.at[step], rx.at[step], xsem.at[step], at(s, step + 1, zh, 0, 0))
+
+    def y_first(step, k):
+        return remote(b1.at[step, (y + k) % 4], ry.at[k - 1, step], ysem.at[step, k - 1], at(s, 0, zh, k, 0))
+
+    pad8 = jnp.zeros((8, 128), F32)
+
+    def join(step):
+        core_copy(step).wait()
+        for half in range(4):
+            rows = own_rows(step, half * 432, 432)
+            both_cores = dko[rows, :] + dkr[rows, :].astype(F32)
+            dko[rows, :] = both_cores
+            if half >= 2:
+                for i in range(2):
+                    piece = jnp.concatenate([both_cores[i * 216 : i * 216 + 216], pad8], axis=0)
+                    b1[step, (half - 2) * 2 + i] = piece.astype(BF16)
+            elif step < 3:
+                b0[step, half * 432 : half * 432 + 432, :] = both_cores.astype(BF16)
+        if step < 3:
+            x_first(step).start()
+        for k in range(1, 4):
+            y_first(step, k).start()
+
+    def then_x(step):
+        return remote(p1.at[step], r2x.at[step], xsem2.at[step], at(s, step + 1, zh, 0, 0))
+
+    def then_y(k):
+        return remote(p0.at[(y + k) % 4], r2y.at[k - 1], ysem2.at[k - 1], at(s, 0, zh, k, 0))
+
+    def sum_y(step):
+        for k in range(1, 4):
+            y_first(step, k).wait()
+        acc = dko[own_rows(step, 864 + y * 216, 216), :]
+        for k in range(3):
+            acc = acc + ry[k, step].astype(F32)[0:216]
+        if step < 3:
+            p1[step] = jnp.concatenate([acc, pad8], axis=0).astype(BF16)
+            then_x(step).start()
+        else:
+            t1[...] = acc
+
+    def sum_x():
+        for step in range(3):
+            x_first(step).wait()
+        for half in range(2):
+            acc = dko[own_rows(3, half * 432, 432), :]
+            for k in range(3):
+                acc = acc + rx[k, half * 432 : half * 432 + 432, :].astype(F32)
+            for i in range(2):
+                piece = acc[i * 216 : i * 216 + 216]
+                t0[half * 2 + i] = piece
+                p0[half * 2 + i] = jnp.concatenate([piece, pad8], axis=0).astype(BF16)
+        for k in range(1, 4):
+            then_y(k).start()
+
     da[...] = convolve(gcol)
 
     @pl.when(s == 3)
     def _():
-        gcen[...] = gc[0:ROWS, :].astype(F32)
+        gcen[...] = gc[0:FR].astype(F32).reshape(ROWS, CH)
         ccol[...] = jnp.zeros_like(ccol)
 
     @pl.when(s < 3)
@@ -431,6 +626,20 @@
             remote(zg.at[pl.ds(0, 8)], ufar, tsem.at[2], cpeer).wait_recv()
             fill_correction(range(4, 6), 1, 32, ufar[...])
 
+
+    @pl.when(s == 0)
+    def _():
+        quarter(0)
+        quarter(1)
+        join(0)
+        quarter(2)
+        join(1)
+        quarter(3)
+        join(2)
+        join(3)
+
+    @pl.when(s < 3)
+    def _():
         da[...] = da[...] - convolve(ccol)
 
     dh3 = (da[...] * dfac[...]).reshape(FR, PX, CH)
@@ -452,10 +661,6 @@
     w = gcen[...] + (rstd[:, None, :] * (dh3 * gain[None])).reshape(ROWS, CH)
     dfac[...] = w
 
-    @pl.when(s == 3)
-    def _():
-        wait_sent(piece_copies(3, w_send, w_recv, w_sems), False)
-
     w_copies = piece_copies(s - 1, w_send, w_recv, w_sems)
 
     @pl.when(s > 0)
@@ -473,67 +678,11 @@
     def _():
         each(w_copies[2], "start")
 
-    def quarter(q):
-        first, last = QUARTERS[q]
-
-        def one(tap, carry):
-            rows = pl.multiple_of(tap * CH, CH)
-            lanes = pl.multiple_of((tap % 9) * CH, CH)
-            frames = pl.multiple_of((2 - tap // 9) * PX, PX)
-            part = jnp.dot(
-                a_t[...], gcol[pl.ds(frames, ROWS), pl.ds(lanes, CH)], preferred_element_type=F32
-            ) - jnp.dot(
-                a_t[...], ccol[pl.ds(frames, ROWS), pl.ds(lanes, CH)], preferred_element_type=F32
-            )
-            dko[pl.ds(rows, CH), :] = jnp.where(core == 0, part[:, :128], part[:, 128:])
-            dks[pl.ds(rows, CH), :] = jnp.where(core == 0, part[:, 128:], part[:, :128]).astype(BF16)
-            return carry
-
-        lax.fori_loop(first, last, one, 0)
-        span = pl.ds(q * 1728, 1728)
-        copy = remote(dks.at[span], dkr.at[span], csem.at[q], cpeer)
-        copy.start()
-        return copy
-
-    pad8 = jnp.zeros((8, 128), F32)
-    y_copies = []
-
-    def x_first(q):
-        return pltpu.make_async_remote_copy(
-            src_ref=b0.at[q], dst_ref=rx.at[x], send_sem=xsem.at[q, 0], recv_sem=xsem.at[x, 1],
-            device_id=at(s, q - x, zh, 0, 0), device_id_type=MESH,
-        )
-
-    def x_first_arrival(source):
-        return pltpu.make_async_remote_copy(
-            src_ref=b0.at[0], dst_ref=rx.at[source], send_sem=xsem.at[0, 0], recv_sem=xsem.at[source, 1],
-            device_id=cpeer, device_id_type=MESH,
-        )
-
-    def join(q, copy):
-        copy.wait()
-        for half in range(4):
-            at0 = q * 1728 + half * 432
-            both_cores = dko[at0 : at0 + 432, :] + dkr[at0 : at0 + 432, :].astype(F32)
-            dko[at0 : at0 + 432, :] = both_cores
-            if half < 2:
-                b0[q, half * 432 : half * 432 + 432, :] = both_cores.astype(BF16)
-            else:
-                for i in range(2):
-                    piece = jnp.concatenate([both_cores[i * 216 : i * 216 + 216], pad8], axis=0)
-                    b1[q, (half - 2) * 2 + i] = piece.astype(BF16)
-
-        @pl.when(x != q)
-        def _():
-            x_first(q).start()
-
-        for k in range(1, 4):
-            y2 = (y + k) % 4
-            c = remote(b1.at[q, y2], ry.at[y, q], ysem.at[q, k - 1], at(s, 0, zh, k, 0))
-            c.start()
-            y_copies.append(c)
-
-    core_copies = [quarter(0), quarter(1)]
+    @pl.when(s > 0)
+    def _():
+        quarter(0)
+        quarter(1)
+
     each(ub_copies, "wait")
     total = jnp.sum(ub[...], axis=0)
     zg[...] = total
@@ -548,7 +697,6 @@
         def _():
             far_sum.start()
 
-    join(0, core_copies[0])
     zg_copy = remote(zg, zgr, zsem.at[3], zpeer)
     zg_copy.start()
     both = spread(total[0:8] / ENTRIES)
@@ -561,61 +709,55 @@
     o_copy.start()
     out_ref[ours] = jnp.where(zh == 0, final[:, 0], final[:, 1])
 
-    core_copies.append(quarter(2))
-    join(1, core_copies[1])
-    core_copies.append(quarter(3))
-    join(2, core_copies[2])
-    join(3, core_copies[3])
+    @pl.when(s > 0)
+    def _():
+        join(0)
+        quarter(2)
+        join(1)
+        quarter(3)
+        join(2)
+        join(3)
+
+    sum_y(0)
+    sum_y(1)
+    sum_y(2)
+    sum_x()
+    sum_y(3)
 
     pad4 = jnp.zeros((4, 128), F32)
 
-    def cut(value, buf, i):
-        buf[i, 0] = jnp.concatenate([value[0:108], pad4], axis=0).astype(BF16)
-        buf[i, 1] = jnp.concatenate([value[108:216], pad4], axis=0).astype(BF16)
-
-    each(y_copies, "wait")
-    for q in range(4):
-        acc = dko[pl.ds(pl.multiple_of(q * 1728 + 864 + y * 216, 8), 216), :]
-        for k in range(1, 4):
-            acc = acc + ry[(y + k) % 4, q].astype(F32)[0:216]
-        cut(acc, p1, q)
-
-    def to_owner(plane_id, i, dc):
-        dx, dy = (i, 0) if plane_id else (0, i)
-        index = (x + i) % 4 if plane_id else (y + i) % 4
-        slot = x if plane_id else y
-        buf = p1 if plane_id else p0
+    def to_owner(plane_id, dc):
         return pltpu.make_async_remote_copy(
-            src_ref=buf.at[index, (core + dc) % 2], dst_ref=r2.at[core, zh, slot],
-            send_sem=psem.at[plane_id, 0, i * 2 + dc], recv_sem=psem.at[zh, 1, i * 2 + dc],
-            device_id=at(s, dx, plane_id, dy, dc), device_id_type=MESH,
+            src_ref=p3.at[plane_id, (core + dc) % 2], dst_ref=r3.at[core, zh],
+            send_sem=psem.at[plane_id, 0, dc], recv_sem=psem.at[zh, 1, dc],
+            device_id=at(s, 0, plane_id, 0, dc), device_id_type=MESH,
         )
 
-    def deliver(plane_id):
-        for i in range(4):
-            for dc in range(2):
-                if (i, dc) != (0, 0):
-                    to_owner(plane_id, i, dc).start()
+    def finish(plane_id):
+        if plane_id:
+            acc = t1[...]
+            for step in range(3):
+                then_x(step).wait()
+                acc = acc + r2x[step].astype(F32)[0:216]
+        else:
+            acc = t0[y]
+            for k in range(1, 4):
+                then_y(k).wait()
+                acc = acc + r2y[k - 1].astype(F32)[0:216]
+        p3[plane_id, 0] = jnp.concatenate([acc[0:108], pad4], axis=0).astype(BF16)
+        p3[plane_id, 1] = jnp.concatenate([acc[108:216], pad4], axis=0).astype(BF16)
+        to_owner(plane_id, 1).start()
 
         @pl.when(zh != plane_id)
         def _():
-            to_owner(plane_id, 0, 0).start()
+            to_owner(plane_id, 0).start()
 
         @pl.when(zh == plane_id)
         def _():
-            buf, slot = (p1, x) if plane_id else (p0, y)
-            r2[core, zh, slot] = buf[slot, core]
-
-    deliver(1)
-    for k in range(1, 4):
-        x_first_arrival((x + k) % 4).wait_recv()
-    for half in range(2):
-        acc = dko[pl.ds(pl.multiple_of(x * 1728 + half * 432, 16), 432), :]
-        for k in range(1, 4):
-            acc = acc + rx[(x + k) % 4, half * 432 : half * 432 + 432, :].astype(F32)
-        cut(acc[0:216], p0, half * 2)
-        cut(acc[216:432], p0, half * 2 + 1)
-    deliver(0)
+            r3[core, zh] = p3[plane_id, core]
+
+    finish(1)
+    finish(0)
 
     zg_copy.wait()
     sums = (zg[...] + zgr[...]) * SCALE
@@ -638,19 +780,13 @@
             xt_far.wait_send()
             far_sum.wait_send()
 
-    for q in range(4):
-
-        @pl.when(x != q)
-        def _():
-            x_first(q).wait_send()
-
     for source in range(2):
-        for j in range(8):
+        for dc in range(2):
             arrival = pltpu.make_async_remote_copy(
-                src_ref=p0.at[0, 0], dst_ref=r2.at[0, 0, 0], send_sem=psem.at[0, 0, j],
-                recv_sem=psem.at[source, 1, j], device_id=cpeer, device_id_type=MESH,
+                src_ref=p3.at[0, 0], dst_ref=r3.at[0, 0], send_sem=psem.at[0, 0, dc],
+                recv_sem=psem.at[source, 1, dc], device_id=cpeer, device_id_type=MESH,
             )
-            if j:
+            if dc:
                 arrival.wait_recv()
             else:
 
@@ -659,22 +795,20 @@
                     arrival.wait_recv()
 
     for half in range(2):
-        acc = jnp.zeros((112, 128), F32)
-        for source in range(2):
-            for i in range(4):
-                acc = acc + r2[half, source, i].astype(F32)
-        kout_ref[:, half * 128 : half * 128 + 128] = acc[0:108] * SCALE
+        value = r3[half, 0].astype(F32) + r3[half, 1].astype(F32)
+        kout_ref[:, 0, half * 128 : half * 128 + 128] = value[0:108] * SCALE
 
     for plane_id in range(2):
-        for i in range(4):
-            for dc in range(2):
-                if (i, dc) != (0, 0):
-                    to_owner(plane_id, i, dc).wait_send()
-                else:
-
-                    @pl.when(zh != plane_id)
-                    def _():
-                        to_owner(plane_id, 0, 0).wait_send()
+        to_owner(plane_id, 1).wait_send()
+
+        @pl.when(zh != plane_id)
+        def _():
+            to_owner(plane_id, 0).wait_send()
+
+
+def write_out(*refs):
+    for source, target in zip(refs[:4], refs[4:]):
+        target[...] = source[...]
 
 
 def on_device(saved_inputs, cotangent, kernels, gains, biases):
@@ -684,11 +818,11 @@
     hbm = pl.BlockSpec(memory_space=pltpu.HBM)
     v = pltpu.VMEM
     dma = pltpu.SemaphoreType.DMA
-    out, kout, gout, bout = pl.pallas_call(
+    made = pl.pallas_call(
         kernel,
         out_shape=(
             jax.ShapeDtypeStruct((8, 32, CH), BF16),
-            jax.ShapeDtypeStruct((108, CH), F32),
+            jax.ShapeDtypeStruct((108, 1, CH), F32),
             jax.ShapeDtypeStruct((1, CH), F32),
             jax.ShapeDtypeStruct((1, CH), F32),
         ),
@@ -696,12 +830,13 @@
         out_specs=[vmem] * 4,
         scratch_shapes=[
             v((8, 32, CH), BF16), v((8, 32, CH), BF16), v((27 * CH, CH), BF16), v((1, CH), F32), v((1, CH), F32),
-            v((FR, 32, CH), BF16), v((FR, 32, CH), BF16), v((FR, 32, CH), BF16), v((FR, 32, CH), BF16),
+            v((FR, 32, CH), BF16), v((8, 128), F32), v((8, 128), F32), v((FR, 32, CH), BF16), v((FR, 32, CH), BF16),
             v((ROWS, CH), F32), v((32, CH), F32),
-            v((ROWS, CH), BF16), v((4, 32, CH), BF16), v((4, 16, CH), BF16),
-            v((ALL, CH), BF16), v((4, 48, CH), BF16), v((2, 4, 16, CH), BF16),
-            v((ROWS, CH), BF16), v((4, 32, CH), BF16), v((4, 16, CH), BF16),
-            v((ALL, CH), BF16), v((4, 48, CH), BF16), v((2, 4, 16, CH), BF16),
+            v((2, 32, CH), BF16), v((64, CH), BF16), v((2, 2, 16, CH), BF16), v((2, 2, 32, CH), BF16),
+            v((FR, 2, 32, CH), BF16), v((4, 32, CH), BF16), v((4, 16, CH), BF16),
+            v((6, 2, 32, CH), BF16), v((4, 48, CH), BF16), v((4, 2, 16, CH), BF16),
+            v((FR, 2, 32, CH), BF16), v((4, 32, CH), BF16), v((4, 16, CH), BF16),
+            v((6, 2, 32, CH), BF16), v((4, 48, CH), BF16), v((4, 2, 16, CH), BF16),
             v((ALL, CH), F32), v((4, 48, CH), F32), v((2, 4, 16, CH), F32), v((60, 24, CH), F32),
             v((ROWS, CH), F32), v((ALL, 9 * CH), BF16), v((ALL, 9 * CH), BF16), v((27 * CH, CH), BF16),
             v((CH, ROWS), BF16), v((ROWS, CH), F32), v((ROWS, CH), F32), v((ROWS, CH), F32),
@@ -709,19 +844,27 @@
             v((8, 128), F32), v((8, 128), F32), v((8, 128), F32), v((2, 8, 128), F32), v((8, CH), F32),
             v((16, 128), F32), v((16, 128), F32),
             v((27 * CH, 128), F32), v((27 * CH, 128), BF16), v((27 * CH, 128), BF16),
-            v((4, 864, 128), BF16), v((4, 4, 224, 128), BF16), v((4, 864, 128), BF16), v((4, 4, 224, 128), BF16),
-            v((4, 2, 112, 128), BF16), v((4, 2, 112, 128), BF16), v((2, 2, 4, 112, 128), BF16),
-            dma((5,)), dma((4, 2)), dma((2, 2)), dma((2, 4, 2)), dma((2, 4, 2)),
+            v((3, 864, 128), BF16), v((4, 4, 224, 128), BF16), v((3, 864, 128), BF16), v((3, 4, 224, 128), BF16),
+            v((4, 224, 128), BF16), v((3, 224, 128), BF16), v((4, 216, 128), F32), v((216, 128), F32),
+            v((3, 224, 128), BF16), v((3, 224, 128), BF16), v((2, 2, 112, 128), BF16), v((2, 2, 112, 128), BF16),
+            dma((6,)), dma((4, 2)), dma((2, 2, 6)), dma((2, 2)), dma((2, 4, 2)), dma((2, 4, 2)),
             dma((2, 2)), dma((2, 4, 2)), dma((2, 4, 2)),
             dma((2,)), dma((16, 2)), dma((2,)), dma((16, 2)), dma((4, 2)), dma((4, 2)),
-            dma((4, 2)), dma((4, 3, 2)), dma((2, 2, 8)),
+            dma((3, 2)), dma((4, 3, 2)), dma((3, 2)), dma((3, 2)), dma((2, 2, 2)),
         ],
         compiler_params=pltpu.CompilerParams(
             collective_id=0, has_side_effects=True, vmem_limit_bytes=VMEM_LIMIT
         ),
         name="blocks",
     )(inputs, seeds, kernels[0], gains, biases)
-    return out.reshape(1, 8, 1, 4, 8, CH), kout[None], gout, bout
+    out, kout, gout, bout = pl.pallas_call(
+        write_out,
+        out_shape=tuple(jax.ShapeDtypeStruct(m.shape, m.dtype) for m in made),
+        in_specs=[vmem] * 4,
+        out_specs=[vmem] * 4,
+        name="write_out",
+    )(*made)
+    return out.reshape(1, 8, 1, 4, 8, CH), kout.reshape(1, 108, CH), gout, bout
 
 
 def solution(mesh):

time: 107 us -> 91.2 us (0.85)
  the two profiles are of different devices: /device:TPU:6 before, /device:TPU:1 now
where the time goes in v3:
time: 91.2 us; the launch traced here: 91.1 us
  Pallas kernels  90.4 us (99%)
    pallas_call x1, Pallas kernels, on_device(): pl.pallas_call(kernel, out_shape=(jax.ShapeDtypeStruct((8, 32, CH), BF16)...  88.7 us

profile of v3, /device:TPU:1, one launch (start us, length us, event | category | flops | bytes accessed | tf_op | source)
XLA Modules:
  0.0 91.1 jit_solution(10702569628875775841)
XLA Ops:
  0.6 88.7 %blocks.1 = (bf16[8,32,256]{2,1,0:T(8,128)(2,1)}, f32[108,1,256]{2,1,0:T(1,128)}, f32[1,256]{1,0:T(1,128)}, f32[1,256]{1,0:T(1,128)}) custom-call(bf16[8,32,256]{2,1,0:T(8,128)(2,1)} %bitcast.8, bf16[8,32,256]{2,1,0:T(8,128)(2,1)} %bitcast.9, bf16[6912,256]{1,0:T(8,128)(2,1)} %bitcast.7, f32[1,256]{1,0:T(1,128)} %gain_hbm.1, f32[1,256]{1,0:T(1,128)} %bias_hbm.1), custom_call_target="tpu_custom_call" | custom-call | tf_op jit(solution)/shard_map/blocks/pallas_call | solution.py:821
  89.4 1.7 %write_out.1 = (bf16[8,32,256]{2,1,0:T(8,128)(2,1)}, f32[108,1,256]{2,1,0:T(1,128)}, f32[1,256]{1,0:T(1,128)}, f32[1,256]{1,0:T(1,128)}) custom-call(bf16[8,32,256]{2,1,0:T(8,128)(2,1)} %get-tuple-element.12.refs_0_, f32[108,1,256]{2,1,0:T(1,128)} %get-tuple-element.13.refs_1_, f32[1,256]{1,0:T(1,128)} %get-tuple-element.14.refs_2_, ...), custom_call_target="tpu_custom_call" | custom-call | tf_op jit(solution)/shard_map/write_out/pallas_call | solution.py:860

commit v4 on v3

--- a/solution.py
+++ b/solution.py
@@ -23,7 +23,10 @@
 SIDES = ((-1, 0), (1, 0), (0, -1), (0, 1))
 CORNERS = ((-1, -1), (-1, 1), (1, -1), (1, 1))
 AROUND = [(dx, dy, dc) for dx in (-1, 0, 1) for dy, dc in ((0, 0), (-1, 1), (0, 1), (1, 1))]
-CHIPS = [(dx, dy) for dx in range(4) for dy in range(4)]
+CHIPS = sorted(
+    ((dx, dy) for dx in range(4) for dy in range(4)),
+    key=lambda d: (d != (0, 0), -min(d[0], 4 - d[0]) - min(d[1], 4 - d[1]), d),
+)
 QUARTER = 1728
 F32 = jnp.float32
 BF16 = jnp.bfloat16
@@ -35,7 +38,7 @@
     x_ref, cot_ref, k_ref, gain_ref, bias_ref,
     xr, xst, xstr, osend, orecv, rf, strip, lrs, rows_s, nooks, lr,
     wc, wh, wn, gc, gh, gn, xwc, xwh, xwn, xgc, xgh, xgn,
-    xc, xs, xn, gp, gcen, gcol, ccol, kt_ref, a_t, xhat, dfac, da,
+    xc, xs, xn, gp, gcen, cols, kt_ref, a_t, xhat, dfac, da, rs,
     sa, sb, ua, ub, unear, ufar, xt, xtr, mom, zg, zgr,
     dko, dks, dkr, b0, b1, rx, ry, p0, p1, t0, t1, r2x, r2y, p3, r3,
     lsem, zsem, dsem, wgs, whs, wns, xgs, xhs, xns, acs, aps, ucs, ups, tsem, csem, xsem, ysem, xsem2, ysem2, psem,
@@ -155,22 +158,37 @@
     xst[...] = tile_sums(theirs)
     xst_copy = remote(xst, xstr, zsem.at[1], zpeer)
     xst_copy.start()
+
+    @pl.when(s == 3)
+    def _():
+        x_copy.start()
+
     own_sums = tile_sums(ours)
 
-    def pack(value, center, sides, corners):
+    def each(copies, what):
+        for c in copies:
+            getattr(c, what)()
+
+    def pack(value, send, copies):
+        center, sides, corners = send
+        near, middle, _ = copies
         rf[...] = value
-        center[...] = value.astype(BF16).reshape(FR, 2, 32, CH)
+        for i, pixel in enumerate((0, 7, 56, 63)):
+            rows = [rf[f * PX + pixel : f * PX + pixel + 1, :] for f in range(FR)]
+            corners[i] = jnp.concatenate(rows + [jnp.zeros((12, CH), F32)], axis=0).astype(BF16)
+        each(near[0:4], "start")
         v4 = value.reshape(FR, 8, 8, CH)
         sides[0] = v4[:, 0].reshape(32, CH).astype(BF16)
         sides[1] = v4[:, 7].reshape(32, CH).astype(BF16)
+        each(near[4:6], "start")
         for i, lead in ((2, 0), (3, 7)):
             for f in range(FR):
                 rows = [rf[f * PX + r * 8 + lead : f * PX + r * 8 + lead + 1, :] for r in range(8)]
                 strip[f * 8 : f * 8 + 8, :] = jnp.concatenate(rows, axis=0)
             sides[i] = strip[...].astype(BF16)
-        for i, pixel in enumerate((0, 7, 56, 63)):
-            rows = [rf[f * PX + pixel : f * PX + pixel + 1, :] for f in range(FR)]
-            corners[i] = jnp.concatenate(rows + [jnp.zeros((12, CH), F32)], axis=0).astype(BF16)
+        each(near[6:8], "start")
+        center[...] = value.astype(BF16).reshape(FR, 2, 32, CH)
+        middle.start()
 
     def piece_copies(sec, send, recv, sems):
         center, sides, corners = send
@@ -190,20 +208,6 @@
             remote(center.at[pl.ds(0, 2)], center_r.at[pl.ds(FR, 2)], gs.at[1], beside(sec, 0, 0, 0))
         )
         return near, middle, far
-
-    def each(copies, what):
-        for c in copies:
-            getattr(c, what)()
-
-    def send_pieces(copies, with_middle):
-        near, middle, far = copies
-        each(near, "start")
-        if with_middle:
-            middle.start()
-
-        @pl.when(zh == 1)
-        def _():
-            each(far, "start")
 
     def wait_sent(copies, with_middle):
         near, middle, far = copies
@@ -306,7 +310,6 @@
                 nooks[i, part] = jnp.concatenate(picks + [jnp.zeros((12, CH), F32)], axis=0).astype(BF16)
         for plane_id in (1, 0):
             each(direct_copies(plane_id)[0], "start")
-        x_copy.start()
 
     def direct_done():
         for plane_id in range(2):
@@ -341,6 +344,19 @@
     def _():
         x_copy.start()
 
+    x_copy.wait()
+    xv = patch(x_ref[ours], xr[...])
+    xhat[...] = xv
+
+    @pl.when(s > 0)
+    def _():
+        copies = piece_copies(s - 1, x_send, x_recv, x_sems)
+        pack(xv, x_send, copies)
+
+        @pl.when(zh == 1)
+        def _():
+            each(copies[2], "start")
+
     k_load.wait()
 
     def flip(i, carry):
@@ -350,43 +366,41 @@
 
     lax.fori_loop(0, 27, flip, 0)
 
-    x_copy.wait()
-    xv = patch(x_ref[ours], xr[...])
-    xhat[...] = xv
-
-    @pl.when(s > 0)
-    def _():
-        pack(xv, xwc, xwh, xwn)
-        send_pieces(piece_copies(s - 1, x_send, x_recv, x_sems), True)
-
-    gain_load.wait()
-    bias_load.wait()
-    each(sb_copies, "wait")
-    xt[...] = jnp.sum(sb[...], axis=0)
     xt_near = remote(xt, xtr.at[0], tsem.at[0], at(s - 1, 0, zh, 0, 0))
     xt_far = remote(xt, xtr.at[1], tsem.at[1], at(s - 1, 0, 0, 0, 0))
-
-    @pl.when(s > 0)
-    def _():
-        xt_near.start()
-
-        @pl.when(zh == 1)
-        def _():
-            xt_far.start()
 
     def moments(total):
         total = spread(total / ENTRIES)
         mean = total[0:4]
         return mean, lax.rsqrt(total[4:8] - mean * mean + EPS)
 
-    mean, rstd = moments(xt[...])
-    gain = gain_ref[...]
-    xh = (xhat[...].reshape(FR, PX, CH) - mean[:, None, :]) * rstd[:, None, :]
-    h = xh * gain[None] + bias_ref[...][None]
-    sg = jax.nn.sigmoid(h)
-    xhat[...] = xh.reshape(ROWS, CH)
-    dfac[...] = (sg * (1.0 + h * (1.0 - sg))).reshape(ROWS, CH)
-    a_t[...] = jnp.transpose((h * sg).reshape(ROWS, CH)).astype(BF16)
+    def prepare():
+        gain_load.wait()
+        bias_load.wait()
+        each(sb_copies, "wait")
+        xt[...] = jnp.sum(sb[...], axis=0)
+        @pl.when(s > 0)
+        def _():
+            xt_near.start()
+
+            @pl.when(zh == 1)
+            def _():
+                xt_far.start()
+
+        mean, rstd = moments(xt[...])
+        gain = gain_ref[...]
+        rs[0:FR, :] = rstd
+        xh = (xhat[...].reshape(FR, PX, CH) - mean[:, None, :]) * rstd[:, None, :]
+        h = xh * gain[None] + bias_ref[...][None]
+        sg = jax.nn.sigmoid(h)
+        xhat[...] = xh.reshape(ROWS, CH)
+        dfac[...] = (sg * (1.0 + h * (1.0 - sg))).reshape(ROWS, CH)
+        act = h * sg
+        a_t[...] = jnp.transpose(jnp.concatenate([act, -act], axis=1).reshape(2 * ROWS, CH)).astype(BF16)
+
+    @pl.when(s < 3)
+    def _():
+        prepare()
 
     @pl.when(s < 3)
     def _():
@@ -420,7 +434,7 @@
 
     edge = (x > 0, x < 3, col > 0, col < 7)
 
-    def columns(frames, center, sides, corners, out):
+    def columns(frames, center, sides, corners, shift):
         top = jnp.where(edge[0], sides[1], 0.0)
         bottom = jnp.where(edge[1], sides[0], 0.0)
         left = jnp.where(edge[2], sides[3], 0.0)
@@ -447,7 +461,7 @@
                 band = gp[base : base + 10, 7 + ox : 15 + ox, :]
                 for oy in range(3):
                     tap = (2 - oy) * 3 + (2 - ox)
-                    out[f * PX : f * PX + PX, tap * CH : tap * CH + CH] = (
+                    cols[f * 2 * PX + shift : f * 2 * PX + shift + PX, tap * CH : tap * CH + CH] = (
                         band[oy : oy + 8].reshape(PX, CH).astype(BF16)
                     )
 
@@ -456,7 +470,7 @@
         columns(
             frames, gc[frames[0] : frames[0] + n].astype(F32),
             [gh[i, row0 : row0 + 8 * n, :].astype(F32) for i in range(4)],
-            [gn[i, part].astype(F32)[0:n] for i in range(4)], gcol,
+            [gn[i, part].astype(F32)[0:n] for i in range(4)], 0,
         )
 
     def fill_correction(frames, part, row0, sums):
@@ -475,60 +489,69 @@
             gcen[...] = gc[0:FR].astype(F32).reshape(ROWS, CH) - center
         columns(
             frames, center, [term(xs[i, row0 : row0 + 8 * n, :], 8) for i in range(4)],
-            [c1 + xn[part, i, 0:n, :] * c2 for i in range(4)], ccol,
+            [c1 + xn[part, i, 0:n, :] * c2 for i in range(4)], PX,
         )
 
-    def convolve(cols):
+    def convolve(shift):
         value = jnp.zeros((ROWS, CH), F32)
         for kt in range(3):
+            starts = [(2 - kt + f) * 2 * PX + shift for f in range(FR)]
             value = value + jnp.dot(
-                cols[(2 - kt) * PX : (2 - kt) * PX + ROWS, :],
+                jnp.concatenate([cols[r : r + PX, :] for r in starts], axis=0),
                 kt_ref[kt * 9 * CH : (kt + 1) * 9 * CH, :],
                 preferred_element_type=F32,
             )
         return value
 
-    near, middle, far = arriving
+    def gather():
+        near, middle, far = arriving
+
+        @pl.when(s == 3)
+        def _():
+            direct_done()
+
+        @pl.when(s < 3)
+        def _():
+            each(near, "wait_recv")
+            middle.wait_recv()
+
+        fill(range(4), 0, 0)
+
+        @pl.when(zh == 0)
+        def _():
+            @pl.when(s < 3)
+            def _():
+                each(far, "wait_recv")
+
+            fill(range(4, 6), 1, 32)
+
+        @pl.when(zh == 1)
+        def _():
+            cols[2 * ROWS :, :] = jnp.zeros((4 * PX, 9 * CH), BF16)
+
+        da[...] = convolve(0)
 
     @pl.when(s == 3)
     def _():
-        direct_done()
+        gather()
+        prepare()
 
     @pl.when(s < 3)
     def _():
-        each(near, "wait_recv")
-        middle.wait_recv()
-
-    fill(range(4), 0, 0)
-
-    @pl.when(zh == 0)
-    def _():
-        @pl.when(s < 3)
-        def _():
-            each(far, "wait_recv")
-
-        fill(range(4, 6), 1, 32)
-
-    @pl.when(zh == 1)
-    def _():
-        gcol[ROWS:, :] = jnp.zeros((2 * PX, 9 * CH), BF16)
-        ccol[ROWS:, :] = jnp.zeros((2 * PX, 9 * CH), BF16)
-
-    def taps(first, last):
-        def one(tap, carry):
-            rows = pl.multiple_of(tap * CH, CH)
-            lanes = pl.multiple_of((tap % 9) * CH, CH)
-            frames = pl.multiple_of((2 - tap // 9) * PX, PX)
-            part = jnp.dot(
-                a_t[...], gcol[pl.ds(frames, ROWS), pl.ds(lanes, CH)], preferred_element_type=F32
-            ) - jnp.dot(
-                a_t[...], ccol[pl.ds(frames, ROWS), pl.ds(lanes, CH)], preferred_element_type=F32
-            )
-            dko[pl.ds(rows, CH), :] = jnp.where(core == 0, part[:, :128], part[:, 128:])
-            dks[pl.ds(rows, CH), :] = jnp.where(core == 0, part[:, 128:], part[:, :128]).astype(BF16)
-            return carry
-
-        lax.fori_loop(first, last, one, 0)
+        gather()
+
+    gain = gain_ref[...]
+    rstd = rs[0:FR, :]
+
+    def one_tap(tap):
+        rows = pl.ds(pl.multiple_of(tap * CH, CH), CH)
+        lanes = pl.multiple_of((tap % 9) * CH, CH)
+        frames = pl.multiple_of((2 - tap // 9) * 2 * PX, 2 * PX)
+        part = jnp.dot(
+            a_t[...], cols[pl.ds(frames, 2 * ROWS), pl.ds(lanes, CH)], preferred_element_type=F32
+        )
+        dko[rows, :] = jnp.where(core == 0, part[:, :128], part[:, 128:])
+        dks[rows, :] = jnp.where(core == 0, part[:, 128:], part[:, :128]).astype(BF16)
 
     def own_rows(step, offset, count):
         q = (x + 1 + step) % 4
@@ -544,12 +567,12 @@
         if step == 0:
             @pl.when(x < 3)
             def _():
-                taps(7 * x + 6, 7 * x + 7)
-
+                one_tap(7 * x + 6)
+
+        for i in range(6):
+            one_tap(7 * q + i)
         if step < 3:
-            taps(7 * q, 7 * q + 7 - q // 3)
-        else:
-            taps(7 * x, 7 * x + 6)
+            one_tap(7 * q + 6 - q // 3)
         core_copy(step).start()
 
     def x_first(step):
@@ -609,12 +632,11 @@
         for k in range(1, 4):
             then_y(k).start()
 
-    da[...] = convolve(gcol)
-
     @pl.when(s == 3)
     def _():
         gcen[...] = gc[0:FR].astype(F32).reshape(ROWS, CH)
-        ccol[...] = jnp.zeros_like(ccol)
+        for f in range(6):
+            cols[f * 2 * PX + PX : f * 2 * PX + 2 * PX, :] = jnp.zeros((PX, 9 * CH), BF16)
 
     @pl.when(s < 3)
     def _():
@@ -640,7 +662,7 @@
 
     @pl.when(s < 3)
     def _():
-        da[...] = da[...] - convolve(ccol)
+        da[...] = da[...] - convolve(PX)
 
     dh3 = (da[...] * dfac[...]).reshape(FR, PX, CH)
     dh_sum = jnp.sum(dh3, axis=1)
@@ -665,9 +687,7 @@
 
     @pl.when(s > 0)
     def _():
-        pack(w, wc, wh, wn)
-        each(w_copies[0], "start")
-        w_copies[1].start()
+        pack(w, w_send, w_copies)
 
     ua_copy.wait()
     ub[chip] = ua[0] + ua[1]
@@ -682,6 +702,17 @@
     def _():
         quarter(0)
         quarter(1)
+
+    def axis_sums():
+        sum_y(0)
+        sum_y(1)
+        sum_y(2)
+        sum_x()
+        sum_y(3)
+
+    @pl.when(s == 0)
+    def _():
+        axis_sums()
 
     each(ub_copies, "wait")
     total = jnp.sum(ub[...], axis=0)
@@ -718,11 +749,9 @@
         join(2)
         join(3)
 
-    sum_y(0)
-    sum_y(1)
-    sum_y(2)
-    sum_x()
-    sum_y(3)
+    @pl.when(s > 0)
+    def _():
+        axis_sums()
 
     pad4 = jnp.zeros((4, 128), F32)
 
@@ -838,8 +867,8 @@
             v((FR, 2, 32, CH), BF16), v((4, 32, CH), BF16), v((4, 16, CH), BF16),
             v((6, 2, 32, CH), BF16), v((4, 48, CH), BF16), v((4, 2, 16, CH), BF16),
             v((ALL, CH), F32), v((4, 48, CH), F32), v((2, 4, 16, CH), F32), v((60, 24, CH), F32),
-            v((ROWS, CH), F32), v((ALL, 9 * CH), BF16), v((ALL, 9 * CH), BF16), v((27 * CH, CH), BF16),
-            v((CH, ROWS), BF16), v((ROWS, CH), F32), v((ROWS, CH), F32), v((ROWS, CH), F32),
+            v((ROWS, CH), F32), v((2 * ALL, 9 * CH), BF16), v((27 * CH, CH), BF16),
+            v((CH, 2 * ROWS), BF16), v((ROWS, CH), F32), v((ROWS, CH), F32), v((ROWS, CH), F32), v((8, CH), F32),
             v((2, 8, 128), F32), v((16, 8, 128), F32), v((2, 16, 128), F32), v((16, 16, 128), F32),
             v((8, 128), F32), v((8, 128), F32), v((8, 128), F32), v((2, 8, 128), F32), v((8, CH), F32),
             v((16, 128), F32), v((16, 128), F32),

time: 91.2 us -> 86.1 us (0.944)
  Pallas kernels: 90.4 us -> 85.3 us
    pallas_call x1, Pallas kernels: 88.7 us -> 83.6 us  [on_device(): pl.pallas_call(kernel, out_shape=(jax.ShapeDtypeStruct((8, 32, CH), BF16)...]
where the time goes in v4:
time: 86.1 us; the launch traced here: 86 us
  Pallas kernels  85.3 us (99%)
    pallas_call x1, Pallas kernels, on_device(): pl.pallas_call(kernel, out_shape=(jax.ShapeDtypeStruct((8, 32, CH), BF16)...  83.6 us

profile of v4, /device:TPU:1, one launch (start us, length us, event | category | flops | bytes accessed | tf_op | source)
XLA Modules:
  0.0 86.0 jit_solution(7798660831996076751)
XLA Ops:
  0.6 83.6 %blocks.1 = (bf16[8,32,256]{2,1,0:T(8,128)(2,1)}, f32[108,1,256]{2,1,0:T(1,128)}, f32[1,256]{1,0:T(1,128)}, f32[1,256]{1,0:T(1,128)}) custom-call(bf16[8,32,256]{2,1,0:T(8,128)(2,1)} %bitcast.8, bf16[8,32,256]{2,1,0:T(8,128)(2,1)} %bitcast.9, bf16[6912,256]{1,0:T(8,128)(2,1)} %bitcast.7, f32[1,256]{1,0:T(1,128)} %gain_hbm.1, f32[1,256]{1,0:T(1,128)} %bias_hbm.1), custom_call_target="tpu_custom_call" | custom-call | tf_op jit(solution)/shard_map/blocks/pallas_call | solution.py:850
  84.3 1.7 %write_out.1 = (bf16[8,32,256]{2,1,0:T(8,128)(2,1)}, f32[108,1,256]{2,1,0:T(1,128)}, f32[1,256]{1,0:T(1,128)}, f32[1,256]{1,0:T(1,128)}) custom-call(bf16[8,32,256]{2,1,0:T(8,128)(2,1)} %get-tuple-element.12.refs_0_, f32[108,1,256]{2,1,0:T(1,128)} %get-tuple-element.13.refs_1_, f32[1,256]{1,0:T(1,128)} %get-tuple-element.14.refs_2_, ...), custom_call_target="tpu_custom_call" | custom-call | tf_op jit(solution)/shard_map/write_out/pallas_call | solution.py:889

commit v5 on v4

--- a/solution.py
+++ b/solution.py
@@ -18,7 +18,7 @@
 ENTRIES = float(64 * 32 * PER_GROUP)
 SCALE = 1.0 / math.sqrt(8 * 64 * 32)
 EPS = 1e-05
-VMEM_LIMIT = 63 * 2**20
+VMEM_LIMIT = 62 * 2**20
 MESH = pl.DeviceIdType.MESH
 SIDES = ((-1, 0), (1, 0), (0, -1), (0, 1))
 CORNERS = ((-1, -1), (-1, 1), (1, -1), (1, 1))
@@ -39,9 +39,9 @@
     xr, xst, xstr, osend, orecv, rf, strip, lrs, rows_s, nooks, lr,
     wc, wh, wn, gc, gh, gn, xwc, xwh, xwn, xgc, xgh, xgn,
     xc, xs, xn, gp, gcen, cols, kt_ref, a_t, xhat, dfac, da, rs,
-    sa, sb, ua, ub, unear, ufar, xt, xtr, mom, zg, zgr,
+    sb, ua, ub, unear, ufar, xt, xtr, mom, zg, zgr,
     dko, dks, dkr, b0, b1, rx, ry, p0, p1, t0, t1, r2x, r2y, p3, r3,
-    lsem, zsem, dsem, wgs, whs, wns, xgs, xhs, xns, acs, aps, ucs, ups, tsem, csem, xsem, ysem, xsem2, ysem2, psem,
+    lsem, zsem, dsem, wgs, whs, wns, xgs, xhs, xns, asem, aps, ucs, ups, tsem, csem, xsem, ysem, xsem2, ysem2, psem,
 ):
     s = lax.axis_index("section")
     t = lax.axis_index("tile")
@@ -113,6 +113,10 @@
     expected = expected + jnp.where(s == 3, 2 * len(AROUND) - 1, 0)
     pl.semaphore_wait(barrier, expected)
 
+    def each(copies, what):
+        for c in copies:
+            getattr(c, what)()
+
     theirs = pl.ds((1 - zh) * FR, FR)
     ours = pl.ds(zh * FR, FR)
     x_copy = remote(x_hbm.at[theirs], xr, zsem.at[0], zpeer)
@@ -155,19 +159,21 @@
         value = x_ref[frames].astype(F32)
         return grouped(jnp.sum(value, axis=1), jnp.sum(value * value, axis=1))
 
-    xst[...] = tile_sums(theirs)
-    xst_copy = remote(xst, xstr, zsem.at[1], zpeer)
-    xst_copy.start()
+    xst[0] = tile_sums(theirs)
+    xst[1] = tile_sums(ours)
+    mine = zh * 2 + core
+    xst_copies = [
+        remote(xst.at[0], xstr.at[mine], asem.at[0], zpeer),
+        remote(xst.at[0], xstr.at[mine], asem.at[1], at(s, 0, 1 - zh, 0, 1)),
+        remote(xst.at[1], xstr.at[mine], asem.at[2], cpeer),
+    ]
+    each(xst_copies, "start")
 
     @pl.when(s == 3)
     def _():
         x_copy.start()
 
-    own_sums = tile_sums(ours)
-
-    def each(copies, what):
-        for c in copies:
-            getattr(c, what)()
+    xstr[mine] = xst[1]
 
     def pack(value, send, copies):
         center, sides, corners = send
@@ -331,12 +337,8 @@
             def _():
                 direct_copies(plane_id)[1].wait_send()
 
-    xst_copy.wait()
-    sa[core] = own_sums + xstr[...]
-    sa_copy = core_sum_copy(sa, acs)
-    sa_copy.start()
-    sa_copy.wait()
-    sb[chip] = sa[0] + sa[1]
+    each(xst_copies, "wait")
+    sb[chip] = jnp.sum(xstr[...], axis=0)
     sb_copies = chip_copies(sb, aps)
     each(sb_copies, "start")
 
@@ -859,7 +861,7 @@
         out_specs=[vmem] * 4,
         scratch_shapes=[
             v((8, 32, CH), BF16), v((8, 32, CH), BF16), v((27 * CH, CH), BF16), v((1, CH), F32), v((1, CH), F32),
-            v((FR, 32, CH), BF16), v((8, 128), F32), v((8, 128), F32), v((FR, 32, CH), BF16), v((FR, 32, CH), BF16),
+            v((FR, 32, CH), BF16), v((2, 8, 128), F32), v((4, 8, 128), F32), v((FR, 32, CH), BF16), v((FR, 32, CH), BF16),
             v((ROWS, CH), F32), v((32, CH), F32),
             v((2, 32, CH), BF16), v((64, CH), BF16), v((2, 2, 16, CH), BF16), v((2, 2, 32, CH), BF16),
             v((FR, 2, 32, CH), BF16), v((4, 32, CH), BF16), v((4, 16, CH), BF16),
@@ -869,7 +871,7 @@
             v((ALL, CH), F32), v((4, 48, CH), F32), v((2, 4, 16, CH), F32), v((60, 24, CH), F32),
             v((ROWS, CH), F32), v((2 * ALL, 9 * CH), BF16), v((27 * CH, CH), BF16),
             v((CH, 2 * ROWS), BF16), v((ROWS, CH), F32), v((ROWS, CH), F32), v((ROWS, CH), F32), v((8, CH), F32),
-            v((2, 8, 128), F32), v((16, 8, 128), F32), v((2, 16, 128), F32), v((16, 16, 128), F32),
+            v((16, 8, 128), F32), v((2, 16, 128), F32), v((16, 16, 128), F32),
             v((8, 128), F32), v((8, 128), F32), v((8, 128), F32), v((2, 8, 128), F32), v((8, CH), F32),
             v((16, 128), F32), v((16, 128), F32),
             v((27 * CH, 128), F32), v((27 * CH, 128), BF16), v((27 * CH, 128), BF16),
@@ -878,7 +880,7 @@
             v((3, 224, 128), BF16), v((3, 224, 128), BF16), v((2, 2, 112, 128), BF16), v((2, 2, 112, 128), BF16),
             dma((6,)), dma((4, 2)), dma((2, 2, 6)), dma((2, 2)), dma((2, 4, 2)), dma((2, 4, 2)),
             dma((2, 2)), dma((2, 4, 2)), dma((2, 4, 2)),
-            dma((2,)), dma((16, 2)), dma((2,)), dma((16, 2)), dma((4, 2)), dma((4, 2)),
+            dma((3, 2)), dma((16, 2)), dma((2,)), dma((16, 2)), dma((4, 2)), dma((4, 2)),
             dma((3, 2)), dma((4, 3, 2)), dma((3, 2)), dma((3, 2)), dma((2, 2, 2)),
         ],
         compiler_params=pltpu.CompilerParams(

time: 86.1 us -> 84.4 us (0.980)
  Pallas kernels: 85.3 us -> 83.6 us
    pallas_call x1, Pallas kernels: 83.6 us -> 81.9 us  [on_device(): pl.pallas_call(kernel, out_shape=(jax.ShapeDtypeStruct((8, 32, CH), BF16)...]
where the time goes in v5:
time: 84.4 us; the launch traced here: 84.2 us
  Pallas kernels  83.6 us (99%)
    pallas_call x1, Pallas kernels, on_device(): pl.pallas_call(kernel, out_shape=(jax.ShapeDtypeStruct((8, 32, CH), BF16)...  81.9 us
    pallas_call x1, Pallas kernels, on_device(): pl.pallas_call(write_out, out_shape=tuple((jax.ShapeDtypeStruct(m.shape,...  1.7 us

profile of v5, /device:TPU:1, one launch (start us, length us, event | category | flops | bytes accessed | tf_op | source)
XLA Modules:
  0.0 84.2 jit_solution(10012262160779691327)
XLA Ops:
  0.6 81.9 %blocks.1 = (bf16[8,32,256]{2,1,0:T(8,128)(2,1)}, f32[108,1,256]{2,1,0:T(1,128)}, f32[1,256]{1,0:T(1,128)}, f32[1,256]{1,0:T(1,128)}) custom-call(bf16[8,32,256]{2,1,0:T(8,128)(2,1)} %bitcast.8, bf16[8,32,256]{2,1,0:T(8,128)(2,1)} %bitcast.9, bf16[6912,256]{1,0:T(8,128)(2,1)} %bitcast.7, f32[1,256]{1,0:T(1,128)} %gain_hbm.1, f32[1,256]{1,0:T(1,128)} %bias_hbm.1), custom_call_target="tpu_custom_call" | custom-call | tf_op jit(solution)/shard_map/blocks/pallas_call | solution.py:852
  82.5 1.7 %write_out.1 = (bf16[8,32,256]{2,1,0:T(8,128)(2,1)}, f32[108,1,256]{2,1,0:T(1,128)}, f32[1,256]{1,0:T(1,128)}, f32[1,256]{1,0:T(1,128)}) custom-call(bf16[8,32,256]{2,1,0:T(8,128)(2,1)} %get-tuple-element.12.refs_0_, f32[108,1,256]{2,1,0:T(1,128)} %get-tuple-element.13.refs_1_, f32[1,256]{1,0:T(1,128)} %get-tuple-element.14.refs_2_, ...), custom_call_target="tpu_custom_call" | custom-call | tf_op jit(solution)/shard_map/write_out/pallas_call | solution.py:891

commit v6 on v5

--- a/solution.py
+++ b/solution.py
@@ -88,37 +88,63 @@
         pl.semaphore_signal(barrier, inc=1, device_id=device, device_id_type=MESH)
 
     plane = [(dx, 0, dy, 0) for dx, dy in CHIPS if (dx, dy) != (0, 0)]
-    plane += [(0, 1, 0, 0), (0, 1, 0, 1), (0, 0, 0, 1)]
-    for dx, z, dy, dc in plane:
-        greet(at(s, dx, (zh + z) % 2, dy, dc))
-
-    @pl.when(s < 3)
+    plane = [(0, 1, 0, 0), (0, 1, 0, 1)] + plane + [(0, 0, 0, 1)]
+    @pl.when(s == 3)
     def _():
         for dx, dy, dc in AROUND:
-            greet(at(s + 1, dx, zh, dy, dc))
-
-        @pl.when(zh == 0)
-        def _():
-            for dx, dy, dc in AROUND:
-                greet(at(s + 1, dx, 1, dy, dc))
-
-    @pl.when(s == 3)
-    def _():
+            greet(at(3, dx, 1 - zh, dy, dc))
         for dx, dy, dc in AROUND:
             if (dx, dy, dc) != (0, 0, 0):
                 greet(at(3, dx, zh, dy, dc))
-            greet(at(3, dx, 1 - zh, dy, dc))
+
+    for dx, z, dy, dc in plane:
+        greet(at(s, dx, (zh + z) % 2, dy, dc))
+
+    @pl.when(s < 3)
+    def _():
+        for dx, dy, dc in AROUND:
+            greet(at(s + 1, dx, zh, dy, dc))
+
+        @pl.when(zh == 0)
+        def _():
+            for dx, dy, dc in AROUND:
+                greet(at(s + 1, dx, 1, dy, dc))
 
     expected = len(plane) + jnp.where(s > 0, (1 + zh) * len(AROUND), 0)
     expected = expected + jnp.where(s == 3, 2 * len(AROUND) - 1, 0)
+    theirs = pl.ds((1 - zh) * FR, FR)
+    ours = pl.ds(zh * FR, FR)
+
+    def indicator(shape, channel_dim):
+        channel = lax.broadcasted_iota(jnp.int32, shape, channel_dim)
+        group = lax.broadcasted_iota(jnp.int32, shape, 1 - channel_dim)
+        return (channel // PER_GROUP == group).astype(F32)
+
+    def grouped(first, second):
+        return jnp.dot(
+            jnp.concatenate([first, second], axis=0), indicator((CH, 128), 0),
+            precision=lax.Precision.HIGHEST, preferred_element_type=F32,
+        )
+
+    def spread(groups):
+        return jnp.dot(
+            groups, indicator((128, CH), 1), precision=lax.Precision.HIGHEST, preferred_element_type=F32
+        )
+
+    x_load.wait()
+
+    def tile_sums(frames):
+        value = x_ref[frames].astype(F32)
+        return grouped(jnp.sum(value, axis=1), jnp.sum(value * value, axis=1))
+
+    xst[0] = tile_sums(theirs)
+    xst[1] = tile_sums(ours)
     pl.semaphore_wait(barrier, expected)
 
     def each(copies, what):
         for c in copies:
             getattr(c, what)()
 
-    theirs = pl.ds((1 - zh) * FR, FR)
-    ours = pl.ds(zh * FR, FR)
     x_copy = remote(x_hbm.at[theirs], xr, zsem.at[0], zpeer)
 
     def patch(own, other):
@@ -128,22 +154,6 @@
         lower = jnp.where(zh == 0, other, own)
         return jnp.concatenate([upper, lower], axis=1).reshape(ROWS, CH)
 
-    def indicator(shape, channel_dim):
-        channel = lax.broadcasted_iota(jnp.int32, shape, channel_dim)
-        group = lax.broadcasted_iota(jnp.int32, shape, 1 - channel_dim)
-        return (channel // PER_GROUP == group).astype(F32)
-
-    def grouped(first, second):
-        return jnp.dot(
-            jnp.concatenate([first, second], axis=0), indicator((CH, 128), 0),
-            precision=lax.Precision.HIGHEST, preferred_element_type=F32,
-        )
-
-    def spread(groups):
-        return jnp.dot(
-            groups, indicator((128, CH), 1), precision=lax.Precision.HIGHEST, preferred_element_type=F32
-        )
-
     def core_sum_copy(buf, pair):
         return remote(buf.at[core], buf.at[core], pair, cpeer)
 
@@ -153,14 +163,6 @@
             for i, (dx, dy) in enumerate(CHIPS) if i
         ]
 
-    x_load.wait()
-
-    def tile_sums(frames):
-        value = x_ref[frames].astype(F32)
-        return grouped(jnp.sum(value, axis=1), jnp.sum(value * value, axis=1))
-
-    xst[0] = tile_sums(theirs)
-    xst[1] = tile_sums(ours)
     mine = zh * 2 + core
     xst_copies = [
         remote(xst.at[0], xstr.at[mine], asem.at[0], zpeer),

time: 84.4 us -> 83.8 us (level)
  no operation moved by 1% of the time
where the time goes in v6:
time: 83.8 us; the launch traced here: 83.7 us
  Pallas kernels  83.1 us (99%)
    pallas_call x1, Pallas kernels, on_device(): pl.pallas_call(kernel, out_shape=(jax.ShapeDtypeStruct((8, 32, CH), BF16)...  81.4 us
    pallas_call x1, Pallas kernels, on_device(): pl.pallas_call(write_out, out_shape=tuple((jax.ShapeDtypeStruct(m.shape,...  1.7 us

profile of v6, /device:TPU:1, one launch (start us, length us, event | category | flops | bytes accessed | tf_op | source)
XLA Modules:
  0.0 83.7 jit_solution(11549492581356992600)
XLA Ops:
  0.6 81.4 %blocks.1 = (bf16[8,32,256]{2,1,0:T(8,128)(2,1)}, f32[108,1,256]{2,1,0:T(1,128)}, f32[1,256]{1,0:T(1,128)}, f32[1,256]{1,0:T(1,128)}) custom-call(bf16[8,32,256]{2,1,0:T(8,128)(2,1)} %bitcast.8, bf16[8,32,256]{2,1,0:T(8,128)(2,1)} %bitcast.9, bf16[6912,256]{1,0:T(8,128)(2,1)} %bitcast.7, f32[1,256]{1,0:T(1,128)} %gain_hbm.1, f32[1,256]{1,0:T(1,128)} %bias_hbm.1), custom_call_target="tpu_custom_call" | custom-call | tf_op jit(solution)/shard_map/blocks/pallas_call | solution.py:854
  82.0 1.7 %write_out.1 = (bf16[8,32,256]{2,1,0:T(8,128)(2,1)}, f32[108,1,256]{2,1,0:T(1,128)}, f32[1,256]{1,0:T(1,128)}, f32[1,256]{1,0:T(1,128)}) custom-call(bf16[8,32,256]{2,1,0:T(8,128)(2,1)} %get-tuple-element.12.refs_0_, f32[108,1,256]{2,1,0:T(1,128)} %get-tuple-element.13.refs_1_, f32[1,256]{1,0:T(1,128)} %get-tuple-element.14.refs_2_, ...), custom_call_target="tpu_custom_call" | custom-call | tf_op jit(solution)/shard_map/write_out/pallas_call | solution.py:893

commit v7 on v6

--- a/solution.py
+++ b/solution.py
@@ -601,7 +601,7 @@
                 b0[step, half * 432 : half * 432 + 432, :] = both_cores.astype(BF16)
         if step < 3:
             x_first(step).start()
-        for k in range(1, 4):
+        for k in (2, 1, 3):
             y_first(step, k).start()
 
     def then_x(step):
@@ -633,7 +633,7 @@
                 piece = acc[i * 216 : i * 216 + 216]
                 t0[half * 2 + i] = piece
                 p0[half * 2 + i] = jnp.concatenate([piece, pad8], axis=0).astype(BF16)
-        for k in range(1, 4):
+        for k in (2, 1, 3):
             then_y(k).start()
 
     @pl.when(s == 3)

time: 83.8 us -> 83.8 us (level)
  no operation moved by 1% of the time
where the time goes in v7:
time: 83.8 us; the launch traced here: 83.7 us
  Pallas kernels  83.1 us (99%)
    pallas_call x1, Pallas kernels, on_device(): pl.pallas_call(kernel, out_shape=(jax.ShapeDtypeStruct((8, 32, CH), BF16)...  81.4 us
    pallas_call x1, Pallas kernels, on_device(): pl.pallas_call(write_out, out_shape=tuple((jax.ShapeDtypeStruct(m.shape,...  1.7 us

profile of v7, /device:TPU:1, one launch (start us, length us, event | category | flops | bytes accessed | tf_op | source)
XLA Modules:
  0.0 83.7 jit_solution(13750481952557407683)
XLA Ops:
  0.6 81.4 %blocks.1 = (bf16[8,32,256]{2,1,0:T(8,128)(2,1)}, f32[108,1,256]{2,1,0:T(1,128)}, f32[1,256]{1,0:T(1,128)}, f32[1,256]{1,0:T(1,128)}) custom-call(bf16[8,32,256]{2,1,0:T(8,128)(2,1)} %bitcast.8, bf16[8,32,256]{2,1,0:T(8,128)(2,1)} %bitcast.9, bf16[6912,256]{1,0:T(8,128)(2,1)} %bitcast.7, f32[1,256]{1,0:T(1,128)} %gain_hbm.1, f32[1,256]{1,0:T(1,128)} %bias_hbm.1), custom_call_target="tpu_custom_call" | custom-call | tf_op jit(solution)/shard_map/blocks/pallas_call | solution.py:854
  82.0 1.7 %write_out.1 = (bf16[8,32,256]{2,1,0:T(8,128)(2,1)}, f32[108,1,256]{2,1,0:T(1,128)}, f32[1,256]{1,0:T(1,128)}, f32[1,256]{1,0:T(1,128)}) custom-call(bf16[8,32,256]{2,1,0:T(8,128)(2,1)} %get-tuple-element.12.refs_0_, f32[108,1,256]{2,1,0:T(1,128)} %get-tuple-element.13.refs_1_, f32[1,256]{1,0:T(1,128)} %get-tuple-element.14.refs_2_, ...), custom_call_target="tpu_custom_call" | custom-call | tf_op jit(solution)/shard_map/write_out/pallas_call | solution.py:893
